TPU v7x, 768 devices: a whole 4x8x12 slice. The times are simulated.
768 devices in a mesh: owner: 32 (over x, y), hst: 24 (over z, core).
Axes of the slice: x: 4, y: 8, z: 12, core: 2. Of those that a mesh axis runs over, the one named last changes fastest.
Arguments:
- dense_input: bfloat16 [196608, 128], P(('owner', 'hst')), may hold values from -6 to 6
- owner_route: int32 [196608, 26, 1], P(('owner', 'hst')), may hold values from 0 to 31; in each aligned block of 6656 rows (0 to 6655, 6656 to 13311, ..., all dimensions but the last counted through in order) at most 416 rows name the same one
- local_row: int32 [196608, 26], P(('owner', 'hst')), may hold values from 0 to 3071
- labels: int32 [196608], P(('owner', 'hst')), may hold values 0 or 1
- table_rows: float32 [98304, 128], P('owner'), may hold values from -6 to 6
- adagrad_state: float32 [98304], P('owner'), may hold values from 1e-05 to 0.001
- cross_down: bfloat16 [3456, 512], replicated, may hold values from -0.109375 to 0.109375
- cross_up: bfloat16 [512, 3456], replicated, may hold values from -0.25 to 0.25
- cross_bias: float32 [3456], replicated, may hold values from -3 to 3
- out_weight: float32 [3456], replicated, may hold values from -0.109375 to 0.109375
Outputs:
- new_rows: float32 [98304, 128], P('owner')
- logits: float32 [196608], P(('owner', 'hst'))
Inputs may be any that keep to these rules, and one draw needn't show every extreme that they name: `owner_route`: among the lookups of one device no owner index appears more than 416 times, and in every draw some device names some owner exactly 416 times.
All inputs are finite; a program needn't handle non-finite values. No bound on the sum of `labels` on one device may be relied on, other than what follows from the above.
Results may differ from a plain program's by a relative error of at most 0.0018.
The roundings to bfloat16 on the way count: a program that leaves them out, or rounds other values in their place, can miss the bound.
Values may be sent and summed in bfloat16 or wider, within the bound.
A program may use at most 64 MiB of HBM per device.

v0:
```python
import jax
import jax.numpy as jnp
from jax import lax
from jax.sharding import PartitionSpec as P

learn_rate = 0.1


def body(
    dense_input,
    owner_route,
    local_row,
    labels,
    table_rows,
    adagrad_state,
    cross_down,
    cross_up,
    cross_bias,
    out_weight,
):
    owners = lax.axis_size("owner")
    samples = dense_input.shape[0]
    emb_width = dense_input.shape[1]
    tables = local_row.shape[1]
    lookups = samples * tables
    capacity = 2 * lookups // owners
    row_count = table_rows.shape[0]
    owner_ids = owner_route.reshape(lookups)
    wanted = local_row.reshape(lookups)
    member = (owner_ids[:, None] == jnp.arange(owners, dtype=jnp.int32)[None, :]).astype(jnp.int32)
    earlier = jnp.cumsum(member, axis=0) - member
    slot_index = owner_ids * capacity + jnp.sum(earlier * member, axis=1)
    requests = jnp.full((owners * capacity,), row_count, jnp.int32).at[slot_index].set(wanted)
    asked_ids = lax.all_to_all(
        requests.reshape(owners, capacity), "owner", split_axis=0, concat_axis=0, tiled=True
    )
    asked_flat = asked_ids.reshape(owners * capacity)
    padded = jnp.concatenate(
        [table_rows.astype(jnp.bfloat16), jnp.zeros((1, emb_width), jnp.bfloat16)], axis=0
    )
    served = padded[asked_flat].reshape(owners, capacity, emb_width)
    arrived = lax.all_to_all(served, "owner", split_axis=0, concat_axis=0, tiled=True)
    fetched = arrived.reshape(owners * capacity, emb_width)[slot_index].reshape(
        samples, tables * emb_width
    )
    joined = jnp.concatenate([dense_input, fetched], axis=1)
    lowrank = jnp.dot(joined, cross_down, preferred_element_type=jnp.float32).astype(jnp.bfloat16)
    mixing = jnp.dot(lowrank, cross_up, preferred_element_type=jnp.float32) + cross_bias[None, :]
    joined_f = joined.astype(jnp.float32)
    crossed = joined_f * (1.0 + mixing)
    logits = jnp.sum(crossed * out_weight[None, :], axis=1)
    logit_grad = jax.nn.sigmoid(logits) - labels.astype(jnp.float32)
    upstream = logit_grad[:, None] * out_weight[None, :]
    scaled = (upstream * joined_f).astype(jnp.bfloat16)
    back_rank = lax.dot_general(
        scaled, cross_up, (((1,), (1,)), ((), ())), preferred_element_type=jnp.float32
    ).astype(jnp.bfloat16)
    emb_down = cross_down[emb_width:, :]
    emb_grad = upstream[:, emb_width:] * (1.0 + mixing[:, emb_width:]) + lax.dot_general(
        back_rank, emb_down, (((1,), (1,)), ((), ())), preferred_element_type=jnp.float32
    )
    emb_grad = emb_grad.astype(jnp.bfloat16).reshape(lookups, emb_width)
    outgoing = jnp.zeros((owners * capacity, emb_width), jnp.bfloat16).at[slot_index].set(emb_grad)
    returned = lax.all_to_all(
        outgoing.reshape(owners, capacity, emb_width),
        "owner",
        split_axis=0,
        concat_axis=0,
        tiled=True,
    )
    partial_value = (
        jnp.zeros((row_count, emb_width), jnp.float32)
        .at[asked_flat]
        .add(returned.reshape(owners * capacity, emb_width).astype(jnp.float32), mode="drop")
    )
    row_grad = lax.psum(partial_value.astype(jnp.bfloat16), "hst").astype(jnp.float32)
    fresh_state = adagrad_state + jnp.mean(row_grad * row_grad, axis=1)
    new_rows = table_rows - learn_rate * row_grad / jnp.sqrt(fresh_state)[:, None]
    return (new_rows, logits)


def solution(mesh):
    in_specs = (
        P(("owner", "hst"), None),
        P(("owner", "hst"), None, None),
        P(("owner", "hst"), None),
        P(("owner", "hst")),
        P("owner", None),
        P("owner"),
        P(),
        P(),
        P(),
        P(),
    )
    out_specs = (P("owner", None), P(("owner", "hst")))
    return jax.shard_map(body, mesh=mesh, in_specs=in_specs, out_specs=out_specs, check_vma=False)
```

profile of v0, /device:TPU:1, one launch (start us, length us, event | category | flops | bytes accessed | tf_op | source)
XLA Modules:
  0.0 641.0 jit_solution(6732593323735027339)
XLA Ops:
  7.2 0.0 copy-start
  7.2 1.5 broadcast_multiply_fusion.1
  8.7 1.5 copy.13
  10.2 1.6 eq.29
  11.8 1.6 eq.25
  13.5 1.5 copy.12
  15.0 1.7 mul.58
  16.6 1.5 copy.15
  18.2 1.6 reshape.163
  19.8 1.7 fusion.20
  21.5 18.6 %reduce-window.6 = s32[32,52,128]{2,1,0:T(8,128)} reduce-window(s32[32,52,128]{2,1,0:T(8,128)} %fusion.20, s32[]{:T(128)} %constant.13.clone.1), window={size=1x1x128 pad=0_0x0_0x127_0}, to_apply=%region_0.0 | reduce-window | flops 27049984 | bytes 1703940 | tf_op jit(solution)/shard_map/reduce-window
  40.1 2.7 slice_reduce_fusion
  42.8 0.9 reduce-window.9
  43.7 1.5 broadcast_add_fusion
  45.2 1.0 fusion.23
  46.2 1.4 fusion.25
  47.6 25.6 %scatter_custom_fusion = s32[13312]{0:T(1024)} fusion(s32[6656]{0:T(1024)} %fusion.25, s32[6656]{0:T(1024)} %reshape.163, s32[]{:T(128)} %constant.11.clone.1), kind=kCustom, calls=%fused_computation.45 | custom fusion | bytes 53760 | tf_op jit(solution)/shard_map/scatter | solution.py:33
  73.2 1.6 all_to_all.12
  74.8 10.6 %all-to-all-start = ((s32[32,1,416]{2,1,0:T(1,128)}), s32[32,1,416]{2,1,0:T(1,128)}, u32[]{:S(2)}, u32[]{:S(2)}) async-start(s32[32,1,416]{2,1,0:T(1,128)} %all_to_all.12), calls=%async_computation | async-start | bytes 131072 | tf_op jit(solution)/shard_map/all_to_all | solution.py:34
  85.4 1.5 convert_element_type.42
  86.9 0.9 concatenate.6
  87.8 6.4 %all-to-all-done = s32[32,1,416]{2,1,0:T(1,128)} async-done(((s32[32,1,416]{2,1,0:T(1,128)}), s32[32,1,416]{2,1,0:T(1,128)}, u32[]{:S(2)}, u32[]{:S(2)}) %all-to-all-start) | async-done | bytes 53280 | tf_op jit(solution)/shard_map/all_to_all | solution.py:34
  94.3 1.6 reduce.2
  95.9 1.6 reshape.136
  97.5 1.5 compare_select_fusion
  99.0 0.6 broadcast_clamp_fusion
  99.6 50.3 %gather_fusion = bf16[13312,128]{1,0:T(8,128)(2,1)} fusion(bf16[3073,128]{1,0:T(8,128)(2,1)} %concatenate.6, s32[13312]{0:T(1024)} %broadcast_clamp_fusion), kind=kCustom, calls=%fused_computation | custom fusion | bytes 6868992 | tf_op jit(solution)/shard_map/gather | solution.py:41
  149.9 4.8 all-to-all-start.1
  154.7 0.2 all-reduce.3.cloned.1.call-start
  155.0 1.4 pad_clamp_fusion
  156.3 1.5 constant_dynamic-update-slice_fusion.1
  157.8 72.0 %all-to-all-done.1 = bf16[32,416,128]{2,1,0:T(8,128)(2,1)} async-done(((bf16[32,416,128]{2,1,0:T(8,128)(2,1)}), bf16[32,416,128]{2,1,0:T(8,128)(2,1)}, u32[]{:S(2)}, u32[]{:S(2)}) %all-to-all-start.1) | async-done | bytes 3407904 | tf_op jit(solution)/shard_map/all_to_all | solution.py:42
  229.8 16.6 %gather_fusion.1 = bf16[6656,128]{1,0:T(8,128)(2,1)} fusion(bf16[13312,128]{1,0:T(8,128)(2,1)} %bitcast.4, s32[7168]{0:T(1024)} %pad_clamp_fusion), kind=kCustom, calls=%fused_computation.1 | custom fusion | bytes 3434496 | tf_op jit(solution)/shard_map/gather | solution.py:43
  246.4 0.0 copy-start.1
  246.4 4.4 reshape.139
  250.7 2.8 constant_dynamic-update-slice_fusion
  253.6 0.0 copy-done
  253.6 0.0 copy-done.1
  253.6 7.6 %fusion.4 = (f32[256]{0:T(256)}, f32[256,3456]{1,0:T(8,128)}) fusion(bf16[256,3456]{1,0:T(8,128)(2,1)} %constant_dynamic-update-slice_fusion, f32[3456]{0:T(1024)S(1)} %copy-done.1, f32[3456]{0:T(1024)} %param.18, bf16[512,3456]{1,0:T(8,128)(2,1)S(1)} %copy-done, bf16[3456,512]{1,0:T(8,128)(2,1)} %param.16), kind=kOutput, calls=%fused_computation.13 | convolution fusion | flops 1817378560 | bytes 12414976 | tf_op jit(solution)/shard_map/dot_general | solution.py:48
  261.2 0.7 divide_subtract_fusion
  261.9 2.1 broadcast_multiply_fusion
  264.0 8.9 %fusion.2 = bf16[256,3328]{1,0:T(8,128)(2,1)} fusion(f32[256,3456]{1,0:T(8,128)} %get-tuple-element.5, f32[256,3456]{1,0:T(8,128)} %broadcast_multiply_fusion, bf16[3456,512]{1,0:T(8,128)(2,1)} %param.16, bf16[512,3456]{1,0:T(8,128)(2,1)S(1)} %copy-done, bf16[256,3456]{1,0:T(8,128)(2,1)} %constant_dynamic-update-slice_fusion), kind=kOutput, calls=%fused_computation.9 | convolution fusion | flops 1784578048 | bytes 20774912 | tf_op jit(solution)/shard_map/dot_general | solution.py:59
  272.9 4.5 reshape.171
  277.4 19.8 %scatter_custom_fusion.1 = bf16[13312,128]{1,0:T(8,128)(2,1)} fusion(s32[6656]{0:T(1024)} %fusion.25, bf16[6656,128]{1,0:T(8,128)(2,1)} %reshape.171, bf16[]{:T(256)} %constant.15.clone.1), kind=kCustom, calls=%fused_computation.22 | custom fusion | bytes 3408384 | tf_op jit(solution)/shard_map/scatter | solution.py:63
  297.2 76.4 %all_to_all.19 = bf16[32,416,128]{2,1,0:T(8,128)(2,1)} all-to-all(bf16[32,416,128]{2,1,0:T(8,128)(2,1)} %bitcast.38), channel_id=1, replica_groups=mesh['owner'=32,'hst'=24] {'owner'}, dimensions={0} | all-to-all | bytes 6815744 | tf_op jit(solution)/shard_map/all_to_all | solution.py:64
  373.6 0.0 copy-start.2
  373.6 73.0 %scatter_custom_fusion.2 = f32[3072,128]{1,0:T(8,128)} fusion(s32[13312]{0:T(1024)} %bitcast.43, bf16[13312,128]{1,0:T(8,128)(2,1)} %bitcast.37, f32[]{:T(128)} %constant.10.clone.1), kind=kCustom, calls=%fused_computation.5 | custom fusion | flops 3407872 | bytes 4981248 | tf_op jit(solution)/shard_map/scatter-add | solution.py:74
  446.6 2.4 convert_element_type.51
  449.0 0.0 all-reduce.3.cloned.1.call-update
  449.0 180.3 %all-reduce.3.cloned.1.call-done = bf16[3072,128]{1,0:T(8,128)(2,1)} async-done(((bf16[3072,128]{1,0:T(8,128)(2,1)}), bf16[3072,128]{1,0:T(8,128)(2,1)}) %all-reduce.3.cloned.1.call-update) | async-done | bytes 786448 | tf_op jit(solution)/shard_map/psum | solution.py:76
  629.3 1.6 fusion.14
  630.9 0.0 copy-done.2
  630.9 3.2 fusion.13
  (1 shorter events, 0.0 us)
Async XLA Ops:
  7.2 246.4 %copy-start = (bf16[512,3456]{1,0:T(8,128)(2,1)S(1)}, bf16[512,3456]{1,0:T(8,128)(2,1)}, u32[]{:S(2)}) copy-start(bf16[512,3456]{1,0:T(8,128)(2,1)} %param.17) | copy-start | bytes 10616836
  74.8 19.5 %all-to-all-start = ((s32[32,1,416]{2,1,0:T(1,128)}), s32[32,1,416]{2,1,0:T(1,128)}, u32[]{:S(2)}, u32[]{:S(2)}) async-start(s32[32,1,416]{2,1,0:T(1,128)} %all_to_all.12), calls=%async_computation | async-start | bytes 131072 | tf_op jit(solution)/shard_map/all_to_all | solution.py:34
  149.9 79.9 %all-to-all-start.1 = ((bf16[32,416,128]{2,1,0:T(8,128)(2,1)}), bf16[32,416,128]{2,1,0:T(8,128)(2,1)}, u32[]{:S(2)}, u32[]{:S(2)}) async-start(bf16[32,416,128]{2,1,0:T(8,128)(2,1)} %bitcast.39), calls=%async_computation.1 | async-start | bytes 6815744 | tf_op jit(solution)/shard_map/all_to_all | solution.py:42
  154.7 474.5 %all-reduce.3.cloned.1.call-start = ((), (), s32[]{:S(2)}) async-start(), calls=%async_computation.3 | async-start | bytes 1572864 | tf_op jit(solution)/shard_map/psum | solution.py:76
  246.4 7.2 %copy-start.1 = (f32[3456]{0:T(1024)S(1)}, f32[3456]{0:T(1024)}, u32[]{:S(2)}) copy-start(f32[3456]{0:T(1024)} %param.19) | copy-start | bytes 41476
  373.6 257.3 %copy-start.2 = (f32[3072]{0:T(1024)S(1)}, f32[3072]{0:T(1024)}, u32[]{:S(2)}) copy-start(f32[3072]{0:T(1024)} %param.15) | copy-start | bytes 36868
Sparse Core Ops, SparseCore 0:
  449.1 180.1 all-reduce.2
where the time goes:
time: 647 us; the launch traced here: 641 us
  waiting for transfers between devices  259 us (40%)
  local copies, waits for them, and re-layouts  143 us (22%)
  other arithmetic  116 us (18%)
  blocking collectives  76.4 us (12%)
  matrix products  16.5 us (3%)
  starting transfers between devices  15.7 us (2%)
  between operations  14.1 us (2%)
    psum x1, waiting for transfers between devices, body(): lax.psum(partial_value.astype(jnp.bfloat16), 'hst').astype(jnp.float32)  180 us
    all_to_all x1, blocking collectives, body(): lax.all_to_all(outgoing.reshape(owners, capacity, emb_width), 'owner', sp...  76.4 us
    scatter-add x1, other arithmetic, body(): partial_value = jnp.zeros((row_count, emb_width), jnp.float32).at[asked_f...  73 us
    all_to_all x1, waiting for transfers between devices, body(): lax.all_to_all(served, 'owner', split_axis=0, concat_axis=0, tiled=True)  72 us
    gather x1, local copies, waits for them, and re-layouts, body(): served = padded[asked_flat].reshape(owners, capacity, emb_width)  50.3 us
    scatter x1, local copies, waits for them, and re-layouts, body(): jnp.full((owners * capacity,), row_count, jnp.int32).at[slot_index]  25.6 us
    another operation x3, other arithmetic  21 us
    scatter x1, local copies, waits for them, and re-layouts, body(): jnp.zeros((owners * capacity, emb_width), jnp.bfloat16).at[slot_index]  19.8 us
  transfers between devices with their start and end apart: 3, of which 3 were waited for; matrix products, arithmetic and copies ran while one was open for 1% of the time, Pallas kernels for 0%

commit v1 on v0

v1 whole, which is shorter than its diff:
```python
import functools
import jax
import jax.numpy as jnp
from jax import lax
from jax.experimental import pallas as pl
from jax.experimental.pallas import tpu as pltpu
from jax.sharding import PartitionSpec as P

XS, YS, ZS, OWNERS = 4, 8, 12, 32
ROWS = 3072
HALF, PAIR, SUB = 1536, 512, 256
RIGHT, LEFT = 16, 15


def place():
    o = lax.axis_index("owner")
    h = lax.axis_index("hst")
    x, y, z, core = o // YS, o % YS, h // 2, h % 2
    diag = (x + y) % 4
    at_a = 4 * y + diag
    at_b = 4 * ((3 * (y - diag + 8)) % 8) + diag
    return o, h, z, core, (at_a, at_b)


def owner_at(cycle, position):
    p = (position + 2 * OWNERS) % OWNERS
    q, r = p // 4, p % 4
    if cycle == 0:
        return ((r - q + 8) % 4) * YS + q
    return (q % 4) * YS + (3 * q + r) % 8


def greet(devices):
    barrier = pltpu.get_barrier_semaphore()
    for d in devices:
        pl.semaphore_signal(barrier, inc=1, device_id=d, device_id_type=pl.DeviceIdType.MESH)
    pl.semaphore_wait(barrier, len(devices))


def send(src, dst, ssem, rsem, device):
    return pltpu.make_async_remote_copy(
        src_ref=src, dst_ref=dst, send_sem=ssem, recv_sem=rsem,
        device_id=device, device_id_type=pl.DeviceIdType.MESH)


STREAMS = [(c, d) for c in (0, 1) for d in (0, 1)]


def gather_kernel(tab, out, own_sem, ring_s, ring_r, sib_s, sib_r, z_s, z_r, zs_s, zs_r):
    o, h, z, core, at = place()
    color = z % 3
    sib = (o, h + 1 - 2 * core)
    up = (o, ((z + 1) % ZS) * 2 + core)
    down = (o, ((z + ZS - 1) % ZS) * 2 + core)
    nxt = [[(owner_at(c, at[c] + 1), h), (owner_at(c, at[c] - 1), h)] for c in (0, 1)]
    greet([sib, up, down, nxt[0][0], nxt[0][1], nxt[1][0], nxt[1][1]])
    base = core * HALF
    pair_row = [base + ((color + 1) % 3) * PAIR, base + ((color + 2) % 3) * PAIR]
    miss_row = [base + color * PAIR, base + color * PAIR + SUB]
    zdev = [up, down]

    own = pltpu.make_async_copy(tab, out.at[pl.ds(o * ROWS, ROWS)], own_sem)
    own.start()

    def source(c, d, s):
        return owner_at(c, at[c] - 1 - s) if d == 0 else owner_at(c, at[c] + 1 + s)

    def rows(owner, row, n):
        return out.at[pl.ds(pl.multiple_of(owner * ROWS + row, SUB), n)]

    def ring(c, d, s, src_ref):
        w = c * 2 + d
        src = source(c, d, s - 1)
        dst = rows(src, pair_row[c], PAIR)
        return send(dst if src_ref is None else src_ref, dst, ring_s.at[w, s], ring_r.at[w, s], nxt[c][d])

    def sibling(c, d, s):
        w = c * 2 + d
        ref = rows(source(c, d, s), pair_row[c], PAIR)
        return send(ref, ref, sib_s.at[w, s], sib_r.at[w, s], sib)

    def zed(c, d, s):
        w = c * 2 + d
        ref = rows(source(c, d, s), pair_row[c] + c * SUB, SUB)
        return send(ref, ref, z_s.at[w, s], z_r.at[w, s], zdev[c])

    def zsib(c, d, s):
        w = c * 2 + d
        ref = rows(source(c, d, s), miss_row[c], SUB)
        return send(ref, ref, zs_s.at[w, s], zs_r.at[w, s], sib)

    for c, d in STREAMS:
        first = tab.at[pl.ds(pl.multiple_of(pair_row[c], SUB), PAIR)]
        ring(c, d, 0, first).start()

    def arrive(c, d, s, last):
        w = c * 2 + d
        ref = rows(source(c, d, s), pair_row[c], PAIR)
        pltpu.make_async_copy(ref, ref, ring_r.at[w, s]).wait()
        if not last:
            ring(c, d, s + 1, None).start()
        zed(c, d, s).start()
        sibling(c, d, s).start()

    def zarrive(c, d, s):
        w = c * 2 + d
        ref = rows(source(c, d, s), miss_row[c], SUB)
        pltpu.make_async_copy(ref, ref, z_r.at[w, s]).wait()
        zsib(c, d, s).start()

    def step(s, _):
        for c, d in STREAMS:
            arrive(c, d, s, False)

        @pl.when(s > 0)
        def _():
            for c, d in STREAMS:
                zarrive(c, d, s - 1)
        return 0

    lax.fori_loop(0, LEFT - 1, step, 0)
    s = LEFT - 1
    for c, d in STREAMS:
        arrive(c, d, s, d == 1)
    for c, d in STREAMS:
        zarrive(c, d, s - 1)
    for c in (0, 1):
        arrive(c, 0, RIGHT - 1, True)
    for c, d in STREAMS:
        zarrive(c, d, s)
    for c in (0, 1):
        zarrive(c, 0, RIGHT - 1)

    def finish(c, d, s):
        w = c * 2 + d
        ring(c, d, s, None).wait_send()
        sibling(c, d, s).wait_send()
        zed(c, d, s).wait_send()
        zsib(c, d, s).wait_send()
        a = rows(source(c, d, s), (1 - core) * HALF, PAIR)
        pltpu.make_async_copy(a, a, sib_r.at[w, s]).wait()
        a = rows(source(c, d, s), (1 - core) * HALF, SUB)
        pltpu.make_async_copy(a, a, zs_r.at[w, s]).wait()

    def end(s, _):
        for c, d in STREAMS:
            finish(c, d, s)
        return 0

    lax.fori_loop(0, LEFT, end, 0)
    for c in (0, 1):
        finish(c, 0, RIGHT - 1)
    own.wait()


def gather_tables(tab):
    return pl.pallas_call(
        gather_kernel,
        out_shape=jax.ShapeDtypeStruct((OWNERS * ROWS, 128), jnp.bfloat16),
        in_specs=[pl.BlockSpec(memory_space=pl.ANY)],
        out_specs=pl.BlockSpec(memory_space=pl.ANY),
        scratch_shapes=[pltpu.SemaphoreType.DMA(())] + [pltpu.SemaphoreType.DMA((4, 16))] * 8,
        compiler_params=pltpu.CompilerParams(collective_id=0, has_side_effects=True),
        name="gather_tables",
    )(tab)


LOOKUPS = 6656
TABLE = OWNERS * ROWS


def scatter_kernel(ids, g, out, acc, gf, stage, sem):
    def clear(i, _):
        acc[pl.ds(pl.multiple_of(i * 512, 512), 512), :] = jnp.zeros((512, 128), jnp.float32)
        return 0
    lax.fori_loop(0, TABLE // 512, clear, 0)

    def widen(i, _):
        r = pl.ds(pl.multiple_of(i * 128, 128), 128)
        gf[r, :] = g[r, :].astype(jnp.float32)
        return 0
    lax.fori_loop(0, LOOKUPS // 128, widen, 0)

    def add(i, _):
        for k in range(8):
            j = i * 8 + k
            row = ids[j]
            acc[pl.ds(row, 1), :] = acc[pl.ds(row, 1), :] + gf[pl.ds(j, 1), :]
        return 0
    lax.fori_loop(0, LOOKUPS // 8, add, 0)

    def copy(i):
        slot = i % 2
        return pltpu.make_async_copy(stage.at[slot], out.at[pl.ds(pl.multiple_of(i * ROWS, ROWS), ROWS)], sem.at[slot])

    def write(i, _):
        @pl.when(i >= 2)
        def _():
            copy(i - 2).wait()

        def narrow(k, _):
            r = pl.multiple_of(k * 256, 256)
            stage[i % 2, pl.ds(r, 256), :] = acc[pl.ds(pl.multiple_of(i * ROWS + r, 256), 256), :].astype(jnp.bfloat16)
            return 0
        lax.fori_loop(0, ROWS // 256, narrow, 0)
        copy(i).start()
        return 0
    lax.fori_loop(0, OWNERS, write, 0)
    copy(OWNERS - 2).wait()
    copy(OWNERS - 1).wait()


def scatter_rows(ids, g):
    return pl.pallas_call(
        scatter_kernel,
        out_shape=jax.ShapeDtypeStruct((TABLE, 128), jnp.bfloat16),
        in_specs=[pl.BlockSpec(memory_space=pltpu.SMEM), pl.BlockSpec(memory_space=pltpu.VMEM)],
        out_specs=pl.BlockSpec(memory_space=pl.ANY),
        scratch_shapes=[
            pltpu.VMEM((TABLE, 128), jnp.float32), pltpu.VMEM((LOOKUPS, 128), jnp.float32),
            pltpu.VMEM((2, ROWS, 128), jnp.bfloat16), pltpu.SemaphoreType.DMA((2,))],
        compiler_params=pltpu.CompilerParams(vmem_limit_bytes=60 * 1024 * 1024),
        name="scatter_rows",
    )(ids, g)


CHUNK = 128
AHEAD = 4


def reduce_kernel(part, out, own_m, own_z, sib_m, sib_z, ring_b, z_b, fin, zr, tot,
                  lm, lz, sm_s, sm_r, sz_s, sz_r, rg_s, rg_r, zz_s, zz_r, c_s, c_r, b_s, b_r, f_s, f_r, t_s):
    o, h, z, core, at = place()
    color = z % 3
    sib = (o, h + 1 - 2 * core)
    zs = [(o, ((z + k) % ZS) * 2 + core) for k in range(ZS)]
    nxt = [[(owner_at(c, at[c] + 1), h), (owner_at(c, at[c] - 1), h)] for c in (0, 1)]
    greet([sib] + zs[1:] + [nxt[0][0], nxt[0][1], nxt[1][0], nxt[1][1]])
    zdev = [zs[ZS - 1], zs[1]]
    pair = [((color + 1) % 3) * PAIR, ((color + 2) % 3) * PAIR]
    miss = [color * PAIR, color * PAIR + SUB]

    def dest(c, d, s):
        return owner_at(c, at[c] + RIGHT - s) if d == 0 else owner_at(c, at[c] - LEFT + s)

    def src(c, d, s, side, row, n):
        return part.at[pl.ds(pl.multiple_of(dest(c, d, s) * ROWS + side * HALF + row, SUB), n)]

    def loads(c, d, s):
        w = c * 2 + d
        other = 1 - core
        return (
            pltpu.make_async_copy(src(c, d, s, core, miss[c], SUB), own_z.at[w, s], lz.at[w, s]),
            send(src(c, d, s, other, miss[c], SUB), sib_z.at[w, s], sz_s.at[w, s], sz_r.at[w, s], sib),
            pltpu.make_async_copy(src(c, d, s, core, pair[c], PAIR), own_m.at[w, s], lm.at[w, s]),
            send(src(c, d, s, other, pair[c], PAIR), sib_m.at[w, s], sm_s.at[w, s], sm_r.at[w, s], sib),
        )

    def fetch(c, d, s):
        for copy in loads(c, d, s):
            copy.start()

    def zcopy(c, d, s):
        w = c * 2 + d
        return send(own_z.at[w, s], z_b.at[w, s], zz_s.at[w, s], zz_r.at[w, s], zdev[c])

    def rcopy(c, d, s):
        w = c * 2 + d
        return send(own_m.at[w, s], ring_b.at[w, s], rg_s.at[w, s], rg_r.at[w, s], nxt[c][d])

    def zpart(c, d, s):
        w = c * 2 + d
        l = loads(c, d, s)
        l[0].wait()
        l[1].wait_recv()

        def add(i, _):
            r = pl.ds(pl.multiple_of(i * 64, 64), 64)
            own_z[w, s, r, :] = (own_z[w, s, r, :].astype(jnp.float32) + sib_z[w, s, r, :].astype(jnp.float32)).astype(jnp.bfloat16)
            return 0
        lax.fori_loop(0, SUB // 64, add, 0)
        zcopy(c, d, s).start()

    def total(c, d, s, more, final=False):
        w = c * 2 + d
        l = loads(c, d, s)
        l[2].wait()
        l[3].wait_recv()
        zcopy(c, d, s).wait_recv()
        for w2, s2, copy in more:
            copy.wait_recv()

        def add(i, _, with_z, first):
            r = pl.ds(pl.multiple_of(first + i * 64, 64), 64)
            t = own_m[w, s, r, :].astype(jnp.float32) + sib_m[w, s, r, :].astype(jnp.float32)
            if with_z:
                t = t + z_b[w, s, pl.ds(pl.multiple_of(i * 64, 64), 64), :].astype(jnp.float32)
            for w2, s2, _copy in more:
                t = t + ring_b[w2, s2, r, :].astype(jnp.float32)
            t = t.astype(jnp.bfloat16)
            if final:
                fin[c, r, :] = t
            else:
                own_m[w, s, r, :] = t
            return 0
        lax.fori_loop(0, SUB // 64, lambda i, x: add(i, x, c == 0, 0), 0)
        lax.fori_loop(0, SUB // 64, lambda i, x: add(i, x, c == 1, SUB), 0)

    FINAL = RIGHT

    def on(c, d, s):
        total(c, d, s, [(c * 2 + d, s - 1, rcopy(c, d, s - 1))])
        rcopy(c, d, s).start()

    for s in range(AHEAD):
        for c, d in STREAMS:
            fetch(c, d, s)
    for s in range(2):
        for c, d in STREAMS:
            zpart(c, d, s)
    for c, d in STREAMS:
        total(c, d, 0, [])
        rcopy(c, d, 0).start()

    def step(s, _):
        @pl.when(s + AHEAD - 1 < LEFT)
        def _():
            for c, d in STREAMS:
                fetch(c, d, s + AHEAD - 1)

        @pl.when(jnp.logical_and(s + AHEAD - 1 >= LEFT, s + AHEAD - 1 <= RIGHT))
        def _():
            for c in (0, 1):
                fetch(c, 0, s + AHEAD - 1)

        @pl.when(s + 1 < LEFT)
        def _():
            for c, d in STREAMS:
                zpart(c, d, s + 1)

        @pl.when(s + 1 >= LEFT)
        def _():
            for c in (0, 1):
                zpart(c, 0, s + 1)
        for c, d in STREAMS:
            on(c, d, s)
        return 0

    lax.fori_loop(1, LEFT, step, 0)
    for c in (0, 1):
        zpart(c, 0, RIGHT)
    for c in (0, 1):
        on(c, 0, RIGHT - 1)
    for c in (1, 0):
        total(c, 0, FINAL, [(c * 2, RIGHT - 1, rcopy(c, 0, RIGHT - 1)), (c * 2 + 1, LEFT - 1, rcopy(c, 1, LEFT - 1))], True)

    hops = [3, 6, 9, 1, 4, 7, 10]

    def scatter(k):
        hop = hops[k]
        to = (z + hop) % ZS
        ref = fin.at[0 if k < 3 else 1, pl.ds(pl.multiple_of((to // 3) * CHUNK, CHUNK), CHUNK)]
        return send(ref, zr.at[k], c_s.at[k], c_r.at[k], zs[hop])
    order = [3, 6, 0, 2, 4, 5, 1]
    for k in order:
        scatter(k).start()
    mine = pl.ds(pl.multiple_of((z // 3) * CHUNK, CHUNK), CHUNK)
    for k in range(7):
        scatter(k).wait_recv()
    t = fin[0, mine, :].astype(jnp.float32)
    for k in range(7):
        t = t + zr[k].astype(jnp.float32)
    tot[...] = t.astype(jnp.bfloat16)

    def chunk_rows(layer):
        return out.at[pl.ds(pl.multiple_of(core * HALF + ((layer % 3 + 1) % 3) * PAIR + (layer // 3) * CHUNK, CHUNK), CHUNK)]

    def spread(k):
        return send(tot, chunk_rows(z), b_s.at[k], b_r.at[k], zs[k])

    def arrived(k):
        ref = chunk_rows((z + ZS - k) % ZS)
        return send(ref, ref, f_s.at[k], f_r.at[k], sib)
    far = [1, 11, 2, 10, 3, 9, 4, 8, 5, 7, 6]
    for k in far:
        spread(k).start()
    first = send(tot, chunk_rows(z), f_s.at[0], f_r.at[0], sib)
    first.start()
    keep = pltpu.make_async_copy(tot, chunk_rows(z), t_s)
    keep.start()
    for k in far:
        ref = chunk_rows((z + ZS - k) % ZS)
        pltpu.make_async_copy(ref, ref, b_r.at[k]).wait()
        arrived(k).start()
    keep.wait()
    first.wait()
    for k in far:
        spread(k).wait_send()
        arrived(k).wait()
    for k in range(7):
        scatter(k).wait_send()

    def end(c, d, s, ring):
        l = loads(c, d, s)
        l[1].wait_send()
        l[3].wait_send()
        zcopy(c, d, s).wait_send()
        if ring:
            rcopy(c, d, s).wait_send()

    def ends(s, _):
        for c, d in STREAMS:
            end(c, d, s, True)
        return 0
    lax.fori_loop(0, LEFT, ends, 0)
    for c in (0, 1):
        end(c, 0, RIGHT - 1, True)
        end(c, 0, RIGHT, False)


def reduce_tables(part):
    bf = jnp.bfloat16
    dma = lambda *n: pltpu.SemaphoreType.DMA(n)
    n = RIGHT + 1
    return pl.pallas_call(
        reduce_kernel,
        out_shape=jax.ShapeDtypeStruct((ROWS, 128), bf),
        in_specs=[pl.BlockSpec(memory_space=pl.ANY)],
        out_specs=pl.BlockSpec(memory_space=pl.ANY),
        scratch_shapes=[
            pltpu.VMEM((4, n, PAIR, 128), bf), pltpu.VMEM((4, n, SUB, 128), bf),
            pltpu.VMEM((4, n, PAIR, 128), bf), pltpu.VMEM((4, n, SUB, 128), bf),
            pltpu.VMEM((4, RIGHT, PAIR, 128), bf), pltpu.VMEM((4, n, SUB, 128), bf),
            pltpu.VMEM((2, PAIR, 128), bf), pltpu.VMEM((7, CHUNK, 128), bf), pltpu.VMEM((CHUNK, 128), bf),
        ] + [dma(4, n)] * 10 + [dma(7)] * 2 + [dma(ZS)] * 4 + [dma()],
        compiler_params=pltpu.CompilerParams(collective_id=1, has_side_effects=True, vmem_limit_bytes=56 * 1024 * 1024),
        name="reduce_tables",
    )(part)


learn_rate = 0.1


def body(
    dense_input,
    owner_route,
    local_row,
    labels,
    table_rows,
    adagrad_state,
    cross_down,
    cross_up,
    cross_bias,
    out_weight,
):
    samples, emb_width = dense_input.shape
    tables = local_row.shape[1]
    lookups = samples * tables
    ids = (owner_route.reshape(samples, tables) * ROWS + local_row).reshape(lookups)
    full = gather_tables(table_rows.astype(jnp.bfloat16))
    fetched = full[ids].reshape(samples, tables * emb_width)
    joined = jnp.concatenate([dense_input, fetched], axis=1)
    lowrank = jnp.dot(joined, cross_down, preferred_element_type=jnp.float32).astype(jnp.bfloat16)
    mixing = jnp.dot(lowrank, cross_up, preferred_element_type=jnp.float32) + cross_bias[None, :]
    joined_f = joined.astype(jnp.float32)
    crossed = joined_f * (1.0 + mixing)
    logits = jnp.sum(crossed * out_weight[None, :], axis=1)
    logit_grad = jax.nn.sigmoid(logits) - labels.astype(jnp.float32)
    upstream = logit_grad[:, None] * out_weight[None, :]
    scaled = (upstream * joined_f).astype(jnp.bfloat16)
    back_rank = lax.dot_general(
        scaled, cross_up, (((1,), (1,)), ((), ())), preferred_element_type=jnp.float32
    ).astype(jnp.bfloat16)
    emb_down = cross_down[emb_width:, :]
    emb_grad = upstream[:, emb_width:] * (1.0 + mixing[:, emb_width:]) + lax.dot_general(
        back_rank, emb_down, (((1,), (1,)), ((), ())), preferred_element_type=jnp.float32
    )
    emb_grad = emb_grad.astype(jnp.bfloat16).reshape(lookups, emb_width)
    row_grad = reduce_tables(scatter_rows(ids, emb_grad)).astype(jnp.float32)
    fresh_state = adagrad_state + jnp.mean(row_grad * row_grad, axis=1)
    new_rows = table_rows - learn_rate * row_grad / jnp.sqrt(fresh_state)[:, None]
    return (new_rows, logits)


def solution(mesh):
    in_specs = (
        P(("owner", "hst"), None),
        P(("owner", "hst"), None, None),
        P(("owner", "hst"), None),
        P(("owner", "hst")),
        P("owner", None),
        P("owner"),
        P(),
        P(),
        P(),
        P(),
    )
    out_specs = (P("owner", None), P(("owner", "hst")))
    return jax.shard_map(body, mesh=mesh, in_specs=in_specs, out_specs=out_specs, check_vma=False)
```

time: 647 us -> 347 us (0.54)
  Pallas kernels: 0 us -> 274 us
  waiting for transfers between devices: 259 us -> 0 us
  other arithmetic: 116 us -> 12.5 us
  local copies, waits for them, and re-layouts: 143 us -> 42.7 us
  blocking collectives: 76.4 us -> 0 us
  starting transfers between devices: 15.7 us -> 0 us
  between operations: 14.1 us -> 0.73 us
    pallas_call x0 -> x3, Pallas kernels: none -> 274 us  [the longest x1 126 us: reduce_tables(): pl.pallas_call(reduce_kernel, out_shape=jax.ShapeDtypeStruct((ROWS, 128),...]
    psum x1 -> x0, waiting for transfers between devices: 180 us -> none  [body(): lax.psum(partial_value.astype(jnp.bfloat16), 'hst').astype(jnp.float32)]
    all_to_all x2 -> x0, waiting for transfers between devices: 78.4 us -> none  [the longest x1 72 us: body(): lax.all_to_all(served, 'owner', split_axis=0, concat_axis=0, tiled=True)]
    all_to_all x1 -> x0, blocking collectives: 76.4 us -> none  [body(): lax.all_to_all(outgoing.reshape(owners, capacity, emb_width), 'owner', sp...]
    scatter-add x1 -> x0, other arithmetic: 73 us -> none  [body(): partial_value = jnp.zeros((row_count, emb_width), jnp.float32).at[asked_f...]
    scatter x2 -> x0, local copies, waits for them, and re-layouts: 45.4 us -> none  [the longest x1 25.6 us: body(): jnp.full((owners * capacity,), row_count, jnp.int32).at[slot_index]]
    gather x2 -> x1, local copies, waits for them, and re-layouts: 66.9 us -> 25.5 us  [body(): fetched = full[ids].reshape(samples, tables * emb_width)]
    another operation x3 -> x0, other arithmetic: 21 us -> none
  transfers between devices with their start and end apart: 3 -> 0, of which waited for: 3 -> 0; matrix products, arithmetic and copies ran while one was open for 1% -> 0% of each run, Pallas kernels for 0% -> 0%
where the time goes in v1:
time: 347 us; the launch traced here: 346 us
  Pallas kernels  274 us (79%)
  local copies, waits for them, and re-layouts  42.7 us (12%)
  matrix products  16.5 us (5%)
  other arithmetic  12.5 us (4%)
    pallas_call x1, Pallas kernels, reduce_tables(): pl.pallas_call(reduce_kernel, out_shape=jax.ShapeDtypeStruct((ROWS, 128),...  126 us
    pallas_call x1, Pallas kernels, gather_tables(): pl.pallas_call(gather_kernel, out_shape=jax.ShapeDtypeStruct((OWNERS * RO...  106 us
    pallas_call x1, Pallas kernels, scatter_rows(): pl.pallas_call(scatter_kernel, out_shape=jax.ShapeDtypeStruct((TABLE, 128...  41.2 us
    gather x1, local copies, waits for them, and re-layouts, body(): fetched = full[ids].reshape(samples, tables * emb_width)  25.5 us
    dot_general x1, matrix products, body(): lax.dot_general(back_rank, emb_down, (((1,), (1,)), ((), ())), preferred_...  8.9 us
    dot_general x1, matrix products, body(): jnp.dot(lowrank, cross_up, preferred_element_type=jnp.float32)  7.62 us

profile of v1, /device:TPU:1, one launch (start us, length us, event | category | flops | bytes accessed | tf_op | source)
XLA Modules:
  0.0 346.1 jit_solution(7538072833124067441)
XLA Ops:
  0.6 0.0 copy-start
  0.6 1.5 bitcast_add_fusion
  2.2 1.5 copy.14
  3.7 1.7 reshape.51
  5.4 0.8 fusion.16
  6.2 0.6 pad_clamp_fusion
  6.8 2.4 convert_element_type.24.tab
  9.2 106.1 %gather_tables.1 = bf16[98304,128]{1,0:T(8,128)(2,1)} custom-call(bf16[3072,128]{1,0:T(8,128)(2,1)} %convert_element_type.24.tab), custom_call_target="tpu_custom_call" | custom-call | tf_op jit(solution)/shard_map/gather_tables/pallas_call | solution.py:157
  115.3 25.5 %gather_fusion = bf16[6656,128]{1,0:T(8,128)(2,1)} fusion(bf16[98304,128]{1,0:T(8,128)(2,1)} %gather_tables.1, s32[7168]{0:T(1024)} %pad_clamp_fusion), kind=kCustom, calls=%fused_computation | custom fusion | bytes 3434496 | tf_op jit(solution)/shard_map/gather | solution.py:461
  140.8 0.0 copy-start.4
  140.8 4.4 %reshape.52 = bf16[256,3328]{1,0:T(8,128)(2,1)} reshape(bf16[6656,128]{1,0:T(8,128)(2,1)} %gather_fusion) | data formatting | bytes 3407872 | tf_op jit(solution)/shard_map/reshape | solution.py:461
  145.2 1.5 constant_dynamic-update-slice_fusion.1
  146.7 2.8 constant_dynamic-update-slice_fusion
  149.5 0.0 copy-done
  149.5 0.0 copy-done.4
  149.5 7.6 %fusion.2 = (f32[256]{0:T(256)}, f32[256,3456]{1,0:T(8,128)}) fusion(bf16[256,3456]{1,0:T(8,128)(2,1)} %constant_dynamic-update-slice_fusion, f32[3456]{0:T(1024)S(1)} %copy-done.4, f32[3456]{0:T(1024)} %param.18, bf16[512,3456]{1,0:T(8,128)(2,1)S(1)} %copy-done, bf16[3456,512]{1,0:T(8,128)(2,1)} %param.16), kind=kOutput, calls=%fused_computation.7 | convolution fusion | flops 1817378560 | bytes 12414976 | tf_op jit(solution)/shard_map/dot_general | solution.py:464
  157.1 0.7 divide_subtract_fusion
  157.8 2.1 broadcast_multiply_fusion
  160.0 8.9 %fusion = bf16[256,3328]{1,0:T(8,128)(2,1)} fusion(f32[256,3456]{1,0:T(8,128)} %get-tuple-element.3, f32[256,3456]{1,0:T(8,128)} %broadcast_multiply_fusion, bf16[3456,512]{1,0:T(8,128)(2,1)} %param.16, bf16[512,3456]{1,0:T(8,128)(2,1)S(1)} %copy-done, bf16[256,3456]{1,0:T(8,128)(2,1)} %constant_dynamic-update-slice_fusion), kind=kOutput, calls=%fused_computation.3 | convolution fusion | flops 1784578048 | bytes 20774912 | tf_op jit(solution)/shard_map/dot_general | solution.py:475
  168.9 0.0 copy-start.3
  168.9 4.5 %reshape.53.g = bf16[6656,128]{1,0:T(8,128)(2,1)} reshape(bf16[256,3328]{1,0:T(8,128)(2,1)} %fusion) | data formatting | bytes 3407872 | tf_op jit(solution)/shard_map/reshape | solution.py:478
  173.4 0.0 copy-done.3
  173.4 0.7 reshape.50.ids
  174.1 41.2 %scatter_rows.1.part = bf16[98304,128]{1,0:T(8,128)(2,1)} custom-call(s32[6656]{0:T(1024)} %reshape.50.ids, bf16[6656,128]{1,0:T(8,128)(2,1)} %reshape.53.g), custom_call_target="tpu_custom_call" | custom-call | tf_op jit(solution)/shard_map/scatter_rows/pallas_call | solution.py:214
  215.3 0.0 copy-start.5
  215.3 0.0 copy-start.2
  215.3 0.0 copy-start.1
  215.4 126.3 %reduce_tables.1 = bf16[3072,128]{1,0:T(8,128)(2,1)} custom-call(bf16[98304,128]{1,0:T(8,128)(2,1)} %scatter_rows.1.part), custom_call_target="tpu_custom_call" | custom-call | tf_op jit(solution)/shard_map/reduce_tables/pallas_call | solution.py:425
  341.7 1.6 fusion.10
  343.3 0.0 copy-done.5
  343.3 0.0 copy-done.2
  343.3 2.8 fusion.9
  346.1 0.0 copy-done.1
  (1 shorter events, 0.0 us)
Async XLA Ops:
  0.6 148.9 %copy-start = (bf16[512,3456]{1,0:T(8,128)(2,1)S(1)}, bf16[512,3456]{1,0:T(8,128)(2,1)}, u32[]{:S(2)}) copy-start(bf16[512,3456]{1,0:T(8,128)(2,1)} %param.17) | copy-start | bytes 10616836
  140.8 8.7 %copy-start.4 = (f32[3456]{0:T(1024)S(1)}, f32[3456]{0:T(1024)}, u32[]{:S(2)}) copy-start(f32[3456]{0:T(1024)} %param.19) | copy-start | bytes 41476
  168.9 4.5 %copy-start.3 = (s32[256,26]{1,0:T(8,128)S(1)}, s32[256,26]{1,0:T(8,128)}, u32[]{:S(2)}) copy-start(s32[256,26]{1,0:T(8,128)} %copy.14) | copy-start | bytes 79876
  215.3 128.0 %copy-start.5 = (f32[3072]{0:T(1024)S(1)}, f32[3072]{0:T(1024)}, u32[]{:S(2)}) copy-start(f32[3072]{0:T(1024)} %param.15) | copy-start | bytes 36868
  215.3 128.0 %copy-start.2 = (f32[3072,128]{1,0:T(8,128)S(1)}, f32[3072,128]{1,0:T(8,128)}, u32[]{:S(2)}) copy-start(f32[3072,128]{1,0:T(8,128)} %param.14) | copy-start | bytes 4718596
  215.3 130.8 %copy-start.1 = (bf16[512,3456]{1,0:T(8,128)(2,1)S(1)}, bf16[512,3456]{1,0:T(8,128)(2,1)}, u32[]{:S(2)}) copy-start(bf16[512,3456]{1,0:T(8,128)(2,1)} %param.17) | copy-start | bytes 10616836

commit v2 on v0

v2 whole, which is shorter than its diff:
```python
import heapq
import jax
import jax.numpy as jnp
from jax import lax
from jax.experimental import pallas as pl
from jax.experimental.pallas import tpu as pltpu
from jax.sharding import PartitionSpec as P

XS, YS, ZS, OWNERS = 4, 8, 12, 32
ROWS = 3072
HALF, PAIR, SUB = 1536, 512, 256
TABLE = OWNERS * ROWS
STEPS = ((1, 0), (-1, 0), (0, 1), (0, -1))


def trees():
    children = [[[] for _ in range(OWNERS)] for _ in range(2)]

    def grow(plan, parent, direction):
        i, j = parent[0] + STEPS[direction][0], parent[1] + STEPS[direction][1]
        children[plan][parent[0] % XS * YS + parent[1] % YS].append((i % XS * YS + j % YS, direction))
        return i, j

    def line(plan, start, direction, count):
        for _ in range(count):
            start = grow(plan, start, direction)
        return start

    def over_x(plan, start, up):
        line(plan, start, 0, up)
        line(plan, start, 1, 3 - up)

    over_x(0, (0, 0), 2)
    for i in range(XS):
        far = line(0, (i, 0), 2, 4 if i == 0 else 3)
        line(0, (i, 0), 3, 3)
        if i == 0:
            over_x(0, far, 1)
    line(1, (0, 0), 2, 3)
    line(1, (0, 0), 3, 4)
    for j in range(YS):
        over_x(1, (0, j), 2 - j % 2)
    return children


def depths(children, n):
    return 1 + max([depths(children, m) for m, _ in children[n]], default=0)


def arrivals(children):
    busy, queue, order = [0.0] * 4, [(0.0, 0, 0, 0), (0.0, 0, 1, 0)], []
    while queue:
        now, _, plan, n = heapq.heappop(queue)
        if n:
            order.append((plan, n))
        for m, direction in sorted(children[plan][n], key=lambda e: -depths(children[plan], e[0])):
            busy[direction] = max(now, busy[direction]) + 2.6
            heapq.heappush(queue, (busy[direction] + 2.5, len(order) * 64 + m, plan, m))
    return order


TREES = trees()
ORDER = arrivals(TREES)


def place():
    o = lax.axis_index("owner")
    h = lax.axis_index("hst")
    x, y, z, core = o // YS, o % YS, h // 2, h % 2
    near = [(((x + i + XS) % XS) * YS + (y + j + YS) % YS, h) for i, j in STEPS]
    owners = [((x + XS - n // YS) % XS) * YS + (y + YS - n % YS) % YS for n in range(OWNERS)]
    return o, h, z, core, near, owners


def greet(devices):
    barrier = pltpu.get_barrier_semaphore()
    for d in devices:
        pl.semaphore_signal(barrier, inc=1, device_id=d, device_id_type=pl.DeviceIdType.MESH)
    pl.semaphore_wait(barrier, len(devices))


def send(src, dst, ssem, rsem, device):
    return pltpu.make_async_remote_copy(
        src_ref=src, dst_ref=dst, send_sem=ssem, recv_sem=rsem,
        device_id=device, device_id_type=pl.DeviceIdType.MESH)


Z_LAG = 6


def gather_kernel(tab, out, own_sem, ring_s, ring_r, sib_s, sib_r, z_s, z_r, zs_s, zs_r):
    o, h, z, core, near, owners = place()
    color = z % 3
    sib = (o, h + 1 - 2 * core)
    zdev = [(o, ((z + 1) % ZS) * 2 + core), (o, ((z + ZS - 1) % ZS) * 2 + core)]
    greet([sib] + zdev + near)
    base = core * HALF
    pair_row = [base + ((color + 1) % 3) * PAIR, base + ((color + 2) % 3) * PAIR]
    miss_row = [base + color * PAIR, base + color * PAIR + SUB]

    own = pltpu.make_async_copy(tab, out.at[pl.ds(pl.multiple_of(o * ROWS, ROWS), ROWS)], own_sem)
    own.start()

    def rows(n, row, count):
        return out.at[pl.ds(pl.multiple_of(owners[n] * ROWS + row, SUB), count)]

    def ring(p, n, m, direction):
        ref = rows(n, pair_row[p], PAIR)
        src = ref if n else tab.at[pl.ds(pl.multiple_of(pair_row[p], SUB), PAIR)]
        return send(src, ref, ring_s.at[p], ring_r.at[p, m], near[direction])

    def sibling(p, n):
        ref = rows(n, pair_row[p], PAIR)
        return send(ref, ref, sib_s.at[p], sib_r.at[p], sib)

    def zed(p, n):
        ref = rows(n, pair_row[p] + p * SUB, SUB)
        return send(ref, ref, z_s.at[p], z_r.at[p, n], zdev[p])

    def zsib(p, n):
        ref = rows(n, miss_row[p], SUB)
        return send(ref, ref, zs_s.at[p], zs_r.at[p], sib)

    def onward(p, n):
        for m, direction in sorted(TREES[p][n], key=lambda e: -depths(TREES[p], e[0])):
            ring(p, n, m, direction).start()

    def await_(ref, sem):
        pltpu.make_async_copy(ref, ref, sem).wait()

    for p in (0, 1):
        onward(p, 0)
    for k in range(len(ORDER) + Z_LAG):
        if k < len(ORDER):
            p, n = ORDER[k]
            await_(rows(n, pair_row[p], PAIR), ring_r.at[p, n])
            onward(p, n)
            zed(p, n).start()
            sibling(p, n).start()
        if k >= Z_LAG:
            p, n = ORDER[k - Z_LAG]
            await_(rows(n, miss_row[p], SUB), z_r.at[p, n])
            zsib(p, n).start()
    whole, half = out.at[pl.ds(0, 31 * PAIR)], out.at[pl.ds(0, 31 * SUB)]
    for p in (0, 1):
        await_(whole, sib_r.at[p])
        await_(half, zs_r.at[p])
        for sem in (ring_s, sib_s):
            await_(whole, sem.at[p])
        for sem in (z_s, zs_s):
            await_(half, sem.at[p])
    own.wait()


def dma(*shape):
    return pltpu.SemaphoreType.DMA(shape)


def gather_tables(tab):
    return pl.pallas_call(
        gather_kernel,
        out_shape=jax.ShapeDtypeStruct((TABLE, 128), jnp.bfloat16),
        in_specs=[pl.BlockSpec(memory_space=pl.ANY)],
        out_specs=pl.BlockSpec(memory_space=pl.ANY),
        scratch_shapes=[dma()] + [dma(2), dma(2, OWNERS), dma(2), dma(2), dma(2), dma(2, OWNERS), dma(2), dma(2)],
        compiler_params=pltpu.CompilerParams(collective_id=2, has_side_effects=True),
        cost_estimate=pl.CostEstimate(flops=0, bytes_accessed=50000000, transcendentals=0),
        name="gather_tables",
    )(tab)


LOOKUPS = 6656


def scatter_kernel(ids, g, out, acc, gf, stage, sem):
    def clear(i, _):
        acc[pl.ds(pl.multiple_of(i * 512, 512), 512), :] = jnp.zeros((512, 128), jnp.float32)
        return 0
    lax.fori_loop(0, TABLE // 512, clear, 0)

    def widen(i, _):
        r = pl.ds(pl.multiple_of(i * 128, 128), 128)
        gf[r, :] = g[r, :].astype(jnp.float32)
        return 0
    lax.fori_loop(0, LOOKUPS // 128, widen, 0)

    def add(i, _):
        for k in range(8):
            j = i * 8 + k
            row = ids[j]
            acc[pl.ds(row, 1), :] = acc[pl.ds(row, 1), :] + gf[pl.ds(j, 1), :]
        return 0
    lax.fori_loop(0, LOOKUPS // 8, add, 0)

    def copy(i):
        slot = i % 2
        return pltpu.make_async_copy(stage.at[slot], out.at[pl.ds(pl.multiple_of(i * ROWS, ROWS), ROWS)], sem.at[slot])

    def write(i, _):
        @pl.when(i >= 2)
        def _():
            copy(i - 2).wait()

        def narrow(k, _):
            r = pl.multiple_of(k * 256, 256)
            stage[i % 2, pl.ds(r, 256), :] = acc[pl.ds(pl.multiple_of(i * ROWS + r, 256), 256), :].astype(jnp.bfloat16)
            return 0
        lax.fori_loop(0, ROWS // 256, narrow, 0)
        copy(i).start()
        return 0
    lax.fori_loop(0, OWNERS, write, 0)
    copy(OWNERS - 2).wait()
    copy(OWNERS - 1).wait()


def scatter_rows(ids, g):
    return pl.pallas_call(
        scatter_kernel,
        out_shape=jax.ShapeDtypeStruct((TABLE, 128), jnp.bfloat16),
        in_specs=[pl.BlockSpec(memory_space=pltpu.SMEM), pl.BlockSpec(memory_space=pltpu.VMEM)],
        out_specs=pl.BlockSpec(memory_space=pl.ANY),
        scratch_shapes=[
            pltpu.VMEM((TABLE, 128), jnp.float32), pltpu.VMEM((LOOKUPS, 128), jnp.float32),
            pltpu.VMEM((2, ROWS, 128), jnp.bfloat16), pltpu.SemaphoreType.DMA((2,))],
        compiler_params=pltpu.CompilerParams(vmem_limit_bytes=60 * 1024 * 1024),
        name="scatter_rows",
    )(ids, g)


CHUNK = 128
LOAD_AHEAD, Z_AHEAD = 20, 10
BACK = [e for e in reversed(ORDER)] + [(0, 0), (1, 0)]


def reduce_kernel(part, out, own_m, own_z, sib_m, sib_z, ring_b, z_b, fin, zr, tot,
                  lm, lz, sm_s, sm_r, sz_s, sz_r, rg_s, rg_r, zz_s, zz_r, c_s, c_r, b_s, b_r, f_s, f_r, t_s):
    o, h, z, core, near, owners = place()
    color = z % 3
    sib = (o, h + 1 - 2 * core)
    zs = [(o, ((z + k) % ZS) * 2 + core) for k in range(ZS)]
    greet([sib] + zs[1:] + near)
    zdev = [zs[ZS - 1], zs[1]]
    pair = [((color + 1) % 3) * PAIR, ((color + 2) % 3) * PAIR]
    miss = [color * PAIR, color * PAIR + SUB]

    def src(n, side, row, count):
        return part.at[pl.ds(pl.multiple_of(owners[n] * ROWS + side * HALF + row, SUB), count)]

    def load_z(p, n):
        return pltpu.make_async_copy(src(n, core, miss[p], SUB), own_z.at[p, n], lz.at[p, n])

    def load_m(p, n):
        return pltpu.make_async_copy(src(n, core, pair[p], PAIR), own_m.at[p, n], lm.at[p, n])

    def give_z(p, n):
        return send(src(n, 1 - core, miss[p], SUB), sib_z.at[p, n], sz_s.at[p], sz_r.at[p, n], sib)

    def give_m(p, n):
        return send(src(n, 1 - core, pair[p], PAIR), sib_m.at[p, n], sm_s.at[p], sm_r.at[p, n], sib)

    def zcopy(p, n):
        return send(own_z.at[p, n], z_b.at[p, n], zz_s.at[p], zz_r.at[p, n], zdev[p])

    def rcopy(p, n, direction):
        return send(own_m.at[p, n], ring_b.at[p, n], rg_s.at[p], rg_r.at[p, n], near[direction ^ 1])

    reached = [{m: d for l in TREES[p] for m, d in l} for p in (0, 1)]

    def fetch(p, n):
        for make in (give_z, load_z, give_m, load_m):
            make(p, n).start()

    def zpart(p, n):
        load_z(p, n).wait()
        give_z(p, n).wait_recv()

        def add(i, _):
            r = pl.ds(pl.multiple_of(i * 128, 128), 128)
            own_z[p, n, r, :] = (own_z[p, n, r, :].astype(jnp.float32) + sib_z[p, n, r, :].astype(jnp.float32)).astype(jnp.bfloat16)
            return 0
        lax.fori_loop(0, SUB // 128, add, 0)
        zcopy(p, n).start()

    def total(p, n):
        load_m(p, n).wait()
        give_m(p, n).wait_recv()
        zcopy(p, n).wait_recv()
        for m, direction in TREES[p][n]:
            rcopy(p, m, direction).wait_recv()

        def add(i, _, with_z, first):
            r = pl.ds(pl.multiple_of(first + i * 128, 128), 128)
            t = own_m[p, n, r, :].astype(jnp.float32) + sib_m[p, n, r, :].astype(jnp.float32)
            if with_z:
                t = t + z_b[p, n, pl.ds(pl.multiple_of(i * 128, 128), 128), :].astype(jnp.float32)
            for m, _direction in TREES[p][n]:
                t = t + ring_b[p, m, r, :].astype(jnp.float32)
            t = t.astype(jnp.bfloat16)
            if n == 0:
                fin[p, r, :] = t
            else:
                own_m[p, n, r, :] = t
            return 0
        lax.fori_loop(0, SUB // 128, lambda i, x: add(i, x, p == 0, 0), 0)
        lax.fori_loop(0, SUB // 128, lambda i, x: add(i, x, p == 1, SUB), 0)
        if n:
            rcopy(p, n, reached[p][n]).start()

    for k in range(-LOAD_AHEAD, len(BACK)):
        if k == -LOAD_AHEAD:
            for e in BACK[:LOAD_AHEAD]:
                fetch(*e)
        if 0 <= k and k + LOAD_AHEAD < len(BACK):
            fetch(*BACK[k + LOAD_AHEAD])
        if -Z_AHEAD <= k and k + Z_AHEAD < len(BACK):
            zpart(*BACK[k + Z_AHEAD])
        if k >= 0:
            total(*BACK[k])

    hops = [3, 6, 9, 1, 4, 7, 10]

    def scatter(k):
        hop = hops[k]
        to = (z + hop) % ZS
        ref = fin.at[0 if k < 3 else 1, pl.ds(pl.multiple_of((to // 3) * CHUNK, CHUNK), CHUNK)]
        return send(ref, zr.at[k], c_s.at[k], c_r.at[k], zs[hop])
    for k in (1, 4, 5, 0, 2, 6, 3):
        scatter(k).start()
    mine = pl.ds(pl.multiple_of((z // 3) * CHUNK, CHUNK), CHUNK)
    for k in range(7):
        scatter(k).wait_recv()
    t = fin[0, mine, :].astype(jnp.float32)
    for k in range(7):
        t = t + zr[k].astype(jnp.float32)
    tot[...] = t.astype(jnp.bfloat16)

    def chunk_rows(layer):
        return out.at[pl.ds(pl.multiple_of(core * HALF + ((layer % 3 + 1) % 3) * PAIR + (layer // 3) * CHUNK, CHUNK), CHUNK)]

    def spread(k):
        return send(tot, chunk_rows(z), b_s.at[k], b_r.at[k], zs[k])

    def arrived(k):
        ref = chunk_rows((z + ZS - k) % ZS)
        return send(ref, ref, f_s.at[k], f_r.at[k], sib)

    far = [6, 5, 7, 4, 8, 3, 9, 2, 10, 1, 11]
    near_first = far[::-1]
    for k in far:
        spread(k).start()
    first = send(tot, chunk_rows(z), f_s.at[0], f_r.at[0], sib)
    first.start()
    keep = pltpu.make_async_copy(tot, chunk_rows(z), t_s)
    keep.start()
    for k in near_first:
        ref = chunk_rows((z + ZS - k) % ZS)
        pltpu.make_async_copy(ref, ref, b_r.at[k]).wait()
        arrived(k).start()
    keep.wait()
    first.wait()
    for k in far:
        spread(k).wait_send()
        arrived(k).wait()
    for k in range(7):
        scatter(k).wait_send()
    for p in (0, 1):
        for ref, sem in (
            (own_z.at[p], sz_s), (own_m.at[p], sm_s), (own_z.at[p], zz_s), (own_m.at[p, pl.ds(1, OWNERS - 1)], rg_s)
        ):
            pltpu.make_async_copy(ref, ref, sem.at[p]).wait()


def reduce_tables(part):
    bf = jnp.bfloat16
    n = OWNERS
    return pl.pallas_call(
        reduce_kernel,
        out_shape=jax.ShapeDtypeStruct((ROWS, 128), bf),
        in_specs=[pl.BlockSpec(memory_space=pl.ANY)],
        out_specs=pl.BlockSpec(memory_space=pl.ANY),
        scratch_shapes=[
            pltpu.VMEM((2, n, PAIR, 128), bf), pltpu.VMEM((2, n, SUB, 128), bf),
            pltpu.VMEM((2, n, PAIR, 128), bf), pltpu.VMEM((2, n, SUB, 128), bf),
            pltpu.VMEM((2, n, PAIR, 128), bf), pltpu.VMEM((2, n, SUB, 128), bf),
            pltpu.VMEM((2, PAIR, 128), bf), pltpu.VMEM((7, CHUNK, 128), bf), pltpu.VMEM((CHUNK, 128), bf),
        ] + [dma(2, n)] * 2 + [dma(2), dma(2, n)] * 4 + [dma(7)] * 2 + [dma(ZS)] * 4 + [dma()],
        compiler_params=pltpu.CompilerParams(collective_id=3, has_side_effects=True, vmem_limit_bytes=56 * 1024 * 1024),
        cost_estimate=pl.CostEstimate(flops=0, bytes_accessed=50000000, transcendentals=0),
        name="reduce_tables",
    )(part)


NT = (((1,), (1,)), ((), ()))


def cross_kernel(dense, fetched, labels, down_hbm, up_hbm, bias, weight, logits, grads, joined, mixed, down, up, sem):
    samples = dense.shape[0]
    take_down = pltpu.make_async_copy(down_hbm, down, sem.at[0])
    take_up = pltpu.make_async_copy(up_hbm, up, sem.at[1])
    take_down.start()
    take_up.start()
    joined[:, 0:128] = dense[...]
    for t in range(26):
        joined[:, 128 * (t + 1):128 * (t + 2)] = fetched[samples * t:samples * (t + 1), :]

    def columns(i, width):
        return pl.ds(pl.multiple_of(i * width, 128), width)

    take_down.wait()

    def first(i, acc):
        c = columns(i, 1152)
        return acc + jnp.dot(joined[:, c], down[c, :], preferred_element_type=jnp.float32)
    lowrank = lax.fori_loop(0, 3, first, jnp.zeros((samples, 512), jnp.float32)).astype(jnp.bfloat16)

    take_up.wait()

    def second(i, acc):
        c = columns(i, 384)
        m = 1.0 + (jnp.dot(lowrank, up[:, c], preferred_element_type=jnp.float32) + bias[:, c])
        mixed[:, c] = m
        v = joined[:, c].astype(jnp.float32) * m * weight[:, c]
        return acc + (v[:, 0:128] + v[:, 128:256] + v[:, 256:384])
    acc = lax.fori_loop(0, 9, second, jnp.zeros((samples, 128), jnp.float32))
    logit = jnp.sum(acc, axis=1, keepdims=True)
    logits[...] = logit
    slope = jax.nn.sigmoid(logit) - labels[...].astype(jnp.float32)

    def third(i, acc):
        c = columns(i, 1152)
        s = (slope * weight[:, c] * joined[:, c].astype(jnp.float32)).astype(jnp.bfloat16)
        return acc + lax.dot_general(s, up[:, c], NT, preferred_element_type=jnp.float32)
    back = lax.fori_loop(0, 3, third, jnp.zeros((samples, 512), jnp.float32)).astype(jnp.bfloat16)

    def fourth(i, _):
        c = pl.ds(pl.multiple_of(128 + i * 256, 128), 256)
        e = slope * weight[:, c] * mixed[:, c] + lax.dot_general(
            back, down[c, :], NT, preferred_element_type=jnp.float32)
        e = e.astype(jnp.bfloat16)
        r = pl.multiple_of(i * 2 * samples, 512)
        grads[pl.ds(r, samples), :] = e[:, 0:128]
        grads[pl.ds(r + samples, samples), :] = e[:, 128:256]
        return 0
    lax.fori_loop(0, 13, fourth, 0)


def cross_layer(dense, fetched, labels, down, up, bias, weight):
    samples = dense.shape[0]
    vmem = pl.BlockSpec(memory_space=pltpu.VMEM)
    return pl.pallas_call(
        cross_kernel,
        out_shape=(
            jax.ShapeDtypeStruct((samples, 1), jnp.float32),
            jax.ShapeDtypeStruct(fetched.shape, jnp.bfloat16)),
        in_specs=[vmem] * 3 + [pl.BlockSpec(memory_space=pl.ANY)] * 2 + [vmem] * 2,
        out_specs=[vmem] * 2,
        scratch_shapes=[pltpu.VMEM((samples, 3456), jnp.bfloat16), pltpu.VMEM((samples, 3456), jnp.float32),
                        pltpu.VMEM(down.shape, jnp.bfloat16), pltpu.VMEM(up.shape, jnp.bfloat16), dma(2)],
        compiler_params=pltpu.CompilerParams(vmem_limit_bytes=60 * 1024 * 1024),
        name="cross_layer",
    )(dense, fetched, labels, down, up, bias, weight)


learn_rate = 0.1


def body(
    dense_input,
    owner_route,
    local_row,
    labels,
    table_rows,
    adagrad_state,
    cross_down,
    cross_up,
    cross_bias,
    out_weight,
):
    samples = dense_input.shape[0]
    tables = local_row.shape[1]
    lookups = samples * tables
    ids = (owner_route.reshape(samples, tables) * ROWS + local_row).T.reshape(lookups)
    fetched = gather_tables(table_rows.astype(jnp.bfloat16))[ids]
    logits, emb_grad = cross_layer(
        dense_input, fetched, labels[:, None], cross_down, cross_up, cross_bias[None, :], out_weight[None, :]
    )
    row_grad = reduce_tables(scatter_rows(ids, emb_grad)).astype(jnp.float32)
    fresh_state = adagrad_state + jnp.mean(row_grad * row_grad, axis=1)
    new_rows = table_rows - learn_rate * row_grad / jnp.sqrt(fresh_state)[:, None]
    return (new_rows, logits.reshape(samples))


def solution(mesh):
    in_specs = (
        P(("owner", "hst"), None),
        P(("owner", "hst"), None, None),
        P(("owner", "hst"), None),
        P(("owner", "hst")),
        P("owner", None),
        P("owner"),
        P(),
        P(),
        P(),
        P(),
    )
    out_specs = (P("owner", None), P(("owner", "hst")))
    return jax.shard_map(body, mesh=mesh, in_specs=in_specs, out_specs=out_specs, check_vma=False)
```

time: 647 us -> 268 us (0.41)
  waiting for transfers between devices: 259 us -> 0 us
  Pallas kernels: 0 us -> 231 us
  local copies, waits for them, and re-layouts: 143 us -> 27.2 us
  other arithmetic: 116 us -> 8.32 us
  blocking collectives: 76.4 us -> 0 us
  matrix products: 16.5 us -> 0 us
  starting transfers between devices: 15.7 us -> 0 us
  between operations: 14.1 us -> 0.77 us
    pallas_call x0 -> x4, Pallas kernels: none -> 231 us  [the longest x1 93.9 us: reduce_tables(): pl.pallas_call(reduce_kernel, out_shape=jax.ShapeDtypeStruct((ROWS, 128),...]
    psum x1 -> x0, waiting for transfers between devices: 180 us -> none  [body(): lax.psum(partial_value.astype(jnp.bfloat16), 'hst').astype(jnp.float32)]
    all_to_all x2 -> x0, waiting for transfers between devices: 78.4 us -> none  [the longest x1 72 us: body(): lax.all_to_all(served, 'owner', split_axis=0, concat_axis=0, tiled=True)]
    all_to_all x1 -> x0, blocking collectives: 76.4 us -> none  [body(): lax.all_to_all(outgoing.reshape(owners, capacity, emb_width), 'owner', sp...]
    scatter-add x1 -> x0, other arithmetic: 73 us -> none  [body(): partial_value = jnp.zeros((row_count, emb_width), jnp.float32).at[asked_f...]
    scatter x2 -> x0, local copies, waits for them, and re-layouts: 45.4 us -> none  [the longest x1 25.6 us: body(): jnp.full((owners * capacity,), row_count, jnp.int32).at[slot_index]]
    gather x2 -> x1, local copies, waits for them, and re-layouts: 66.9 us -> 24.5 us  [body(): fetched = gather_tables(table_rows.astype(jnp.bfloat16))[ids]]
    another operation x3 -> x0, other arithmetic: 21 us -> none
  transfers between devices with their start and end apart: 3 -> 0, of which waited for: 3 -> 0; matrix products, arithmetic and copies ran while one was open for 1% -> 0% of each run, Pallas kernels for 0% -> 0%
where the time goes in v2:
time: 268 us
  Pallas kernels  231 us (86%)
  local copies, waits for them, and re-layouts  27.2 us (10%)
  other arithmetic  8.32 us (3%)
    pallas_call x1, Pallas kernels, reduce_tables(): pl.pallas_call(reduce_kernel, out_shape=jax.ShapeDtypeStruct((ROWS, 128),...  93.9 us
    pallas_call x1, Pallas kernels, gather_tables(): pl.pallas_call(gather_kernel, out_shape=jax.ShapeDtypeStruct((TABLE, 128)...  81.5 us
    pallas_call x1, Pallas kernels, scatter_rows(): pl.pallas_call(scatter_kernel, out_shape=jax.ShapeDtypeStruct((TABLE, 128...  41.2 us
    gather x1, local copies, waits for them, and re-layouts, body(): fetched = gather_tables(table_rows.astype(jnp.bfloat16))[ids]  24.5 us
    pallas_call x1, Pallas kernels, cross_layer(): pl.pallas_call(cross_kernel, out_shape=(jax.ShapeDtypeStruct((samples, 1)...  14.7 us

profile of v2, /device:TPU:1, one launch (start us, length us, event | category | flops | bytes accessed | tf_op | source)
XLA Modules:
  0.0 267.6 jit_solution(1427538483113911720)
XLA Ops:
  0.6 0.8 fusion.4
  1.4 0.1 fusion.3
  1.5 2.4 convert_element_type.6.tab
  3.9 81.5 %gather_tables.1 = bf16[98304,128]{1,0:T(8,128)(2,1)} custom-call(bf16[3072,128]{1,0:T(8,128)(2,1)} %convert_element_type.6.tab), custom_call_target="tpu_custom_call" | custom-call | bytes 50000000 | tf_op jit(solution)/shard_map/gather_tables/pallas_call | solution.py:160
  85.4 0.0 copy-start.5
  85.4 0.0 copy-start.2
  85.4 0.0 copy-start.3
  85.5 24.5 %gather_fusion = bf16[6656,128]{1,0:T(8,128)(2,1)} fusion(bf16[98304,128]{1,0:T(8,128)(2,1)} %gather_tables.1, s32[7168]{0:T(1024)S(1)} %pad_clamp_fusion), kind=kCustom, calls=%fused_computation | custom fusion | bytes 3434496 | tf_op jit(solution)/shard_map/gather | solution.py:483
  110.0 0.0 copy-done.5
  110.0 0.8 copy.14.labels
  110.8 0.0 copy-done.2
  110.8 0.6 broadcast_in_dim.12.bias
  111.4 0.0 copy-done.3
  111.4 0.6 broadcast_in_dim.13.weight
  112.0 14.7 %cross_layer.1 = (f32[256,1]{1,0:T(8,128)}, bf16[6656,128]{1,0:T(8,128)(2,1)}) custom-call(bf16[256,128]{1,0:T(8,128)(2,1)} %dense.1, bf16[6656,128]{1,0:T(8,128)(2,1)} %gather_fusion, s32[256,1]{1,0:T(8,128)} %copy.14.labels, bf16[3456,512]{1,0:T(8,128)(2,1)} %down_hbm.1, bf16[512,3456]{1,0:T(8,128)(2,1)} %up_hbm.1, f32[1,3456]{1,0:T(1,128)} %broadcast_in_dim.12.bias, ...), custom_call_target="tpu_custom_call" | custom-call | tf_op jit(solution)/shard_map/cross_layer/pallas_call | solution.py:450
  126.7 0.6 reshape.44.ids
  127.3 41.2 %scatter_rows.1.part = bf16[98304,128]{1,0:T(8,128)(2,1)} custom-call(s32[6656]{0:T(1024)} %reshape.44.ids, bf16[6656,128]{1,0:T(8,128)(2,1)} %get-tuple-element.4.g), custom_call_target="tpu_custom_call" | custom-call | tf_op jit(solution)/shard_map/scatter_rows/pallas_call | solution.py:217
  168.5 0.0 copy-start.4
  168.5 0.0 copy-start
  168.5 93.9 %reduce_tables.1 = bf16[3072,128]{1,0:T(8,128)(2,1)} custom-call(bf16[98304,128]{1,0:T(8,128)(2,1)} %scatter_rows.1.part), custom_call_target="tpu_custom_call" | custom-call | bytes 50000000 | tf_op jit(solution)/shard_map/reduce_tables/pallas_call | solution.py:376
  262.4 1.6 fusion.2
  264.1 0.0 copy-done.4
  264.1 0.0 copy-done
  264.1 0.0 copy-start.1
  264.1 2.8 %fusion.1 = f32[3072,128]{1,0:T(8,128)} fusion(f32[3072,128]{1,0:T(8,128)S(1)} %copy-done, bf16[3072,128]{1,0:T(8,128)(2,1)} %reduce_tables.1, f32[3072]{0:T(1024)S(1)} %add_sqrt_fusion), kind=kLoop, calls=%fused_computation.4 | loop fusion | flops 1572864 | bytes 3944448 | tf_op jit(solution)/shard_map/sub | solution.py:489
  266.9 0.0 copy-done.1
  266.9 0.7 reduce.1
  (3 shorter events, 0.0 us)
Async XLA Ops:
  85.4 24.6 %copy-start.5 = (s32[256]{0:T(256)S(1)}, s32[256]{0:T(256)}, u32[]{:S(2)}) copy-start(s32[256]{0:T(256)} %param.13) | copy-start | bytes 3076
  85.4 25.4 %copy-start.2 = (f32[3456]{0:T(1024)S(1)}, f32[3456]{0:T(1024)}, u32[]{:S(2)}) copy-start(f32[3456]{0:T(1024)} %param.18) | copy-start | bytes 41476
  85.4 25.9 %copy-start.3 = (f32[3456]{0:T(1024)S(1)}, f32[3456]{0:T(1024)}, u32[]{:S(2)}) copy-start(f32[3456]{0:T(1024)} %param.19) | copy-start | bytes 41476
  168.5 95.6 %copy-start.4 = (f32[3072]{0:T(1024)S(1)}, f32[3072]{0:T(1024)}, u32[]{:S(2)}) copy-start(f32[3072]{0:T(1024)} %param.15) | copy-start | bytes 36868
  168.5 95.6 %copy-start = (f32[3072,128]{1,0:T(8,128)S(1)}, f32[3072,128]{1,0:T(8,128)}, u32[]{:S(2)}) copy-start(f32[3072,128]{1,0:T(8,128)} %param.14) | copy-start | bytes 4718596
  264.1 2.8 %copy-start.1 = (f32[256,1]{1,0:T(8,128)S(1)}, f32[256,1]{1,0:T(8,128)}, u32[]{:S(2)}) copy-start(f32[256,1]{1,0:T(8,128)} %get-tuple-element.5) | copy-start | bytes 3076

commit v3 on v2

--- a/solution.py
+++ b/solution.py
@@ -47,20 +47,33 @@
     return 1 + max([depths(children, m) for m, _ in children[n]], default=0)
 
 
-def arrivals(children):
-    busy, queue, order = [0.0] * 4, [(0.0, 0, 0, 0), (0.0, 0, 1, 0)], []
-    while queue:
-        now, _, plan, n = heapq.heappop(queue)
-        if n:
-            order.append((plan, n))
-        for m, direction in sorted(children[plan][n], key=lambda e: -depths(children[plan], e[0])):
-            busy[direction] = max(now, busy[direction]) + 2.6
-            heapq.heappush(queue, (busy[direction] + 2.5, len(order) * 64 + m, plan, m))
-    return order
+TIME, DELAY = 2.85, 4.0
+
+
+def schedule(children):
+    waiting, busy, events, steps = [[] for _ in STEPS], [False] * 4, [(0.0, 0, 0, 0), (0.0, 1, 1, 0)], []
+    while events:
+        now, _, plan, n = heapq.heappop(events)
+        if plan < 0:
+            busy[n] = False
+        else:
+            if n:
+                steps.append((now, 0, len(steps), (plan, n)))
+            for m, direction in children[plan][n]:
+                heapq.heappush(waiting[direction], (-depths(children[plan], m), now, len(steps), m, plan, n))
+        for direction in range(4):
+            if waiting[direction] and not busy[direction]:
+                _, ready, _, m, p, parent = heapq.heappop(waiting[direction])
+                busy[direction] = True
+                steps.append((max(ready, now - TIME), 1, len(steps), (p, parent, m, direction)))
+                heapq.heappush(events, (now + TIME, 1000 + direction, -1, direction))
+                heapq.heappush(events, (now + TIME + DELAY, 2000 + len(steps), p, m))
+    return [step[3] for step in sorted(steps)]
 
 
 TREES = trees()
-ORDER = arrivals(TREES)
+SCHEDULE = schedule(TREES)
+ORDER = [step for step in SCHEDULE if len(step) == 2]
 
 
 def place():
@@ -121,26 +134,27 @@
         ref = rows(n, miss_row[p], SUB)
         return send(ref, ref, zs_s.at[p], zs_r.at[p], sib)
 
-    def onward(p, n):
-        for m, direction in sorted(TREES[p][n], key=lambda e: -depths(TREES[p], e[0])):
-            ring(p, n, m, direction).start()
-
     def await_(ref, sem):
         pltpu.make_async_copy(ref, ref, sem).wait()
 
-    for p in (0, 1):
-        onward(p, 0)
-    for k in range(len(ORDER) + Z_LAG):
-        if k < len(ORDER):
-            p, n = ORDER[k]
-            await_(rows(n, pair_row[p], PAIR), ring_r.at[p, n])
-            onward(p, n)
-            zed(p, n).start()
-            sibling(p, n).start()
-        if k >= Z_LAG:
-            p, n = ORDER[k - Z_LAG]
-            await_(rows(n, miss_row[p], SUB), z_r.at[p, n])
-            zsib(p, n).start()
+    def from_z(p, n):
+        await_(rows(n, miss_row[p], SUB), z_r.at[p, n])
+        zsib(p, n).start()
+
+    came = []
+    for step in SCHEDULE:
+        if len(step) == 4:
+            ring(*step).start()
+            continue
+        p, n = step
+        await_(rows(n, pair_row[p], PAIR), ring_r.at[p, n])
+        came.append(step)
+        zed(p, n).start()
+        sibling(p, n).start()
+        if len(came) > Z_LAG:
+            from_z(*came[-1 - Z_LAG])
+    for step in came[-Z_LAG:]:
+        from_z(*step)
     whole, half = out.at[pl.ds(0, 31 * PAIR)], out.at[pl.ds(0, 31 * SUB)]
     for p in (0, 1):
         await_(whole, sib_r.at[p])
@@ -174,9 +188,9 @@
 
 def scatter_kernel(ids, g, out, acc, gf, stage, sem):
     def clear(i, _):
-        acc[pl.ds(pl.multiple_of(i * 512, 512), 512), :] = jnp.zeros((512, 128), jnp.float32)
+        acc[pl.ds(pl.multiple_of(i * 1024, 1024), 1024), :] = jnp.zeros((1024, 128), jnp.float32)
         return 0
-    lax.fori_loop(0, TABLE // 512, clear, 0)
+    lax.fori_loop(0, TABLE // 1024, clear, 0)
 
     def widen(i, _):
         r = pl.ds(pl.multiple_of(i * 128, 128), 128)
@@ -185,12 +199,12 @@
     lax.fori_loop(0, LOOKUPS // 128, widen, 0)
 
     def add(i, _):
-        for k in range(8):
-            j = i * 8 + k
+        for k in range(16):
+            j = i * 16 + k
             row = ids[j]
             acc[pl.ds(row, 1), :] = acc[pl.ds(row, 1), :] + gf[pl.ds(j, 1), :]
         return 0
-    lax.fori_loop(0, LOOKUPS // 8, add, 0)
+    lax.fori_loop(0, LOOKUPS // 16, add, 0)
 
     def copy(i):
         slot = i % 2
@@ -202,10 +216,10 @@
             copy(i - 2).wait()
 
         def narrow(k, _):
-            r = pl.multiple_of(k * 256, 256)
-            stage[i % 2, pl.ds(r, 256), :] = acc[pl.ds(pl.multiple_of(i * ROWS + r, 256), 256), :].astype(jnp.bfloat16)
+            r = pl.multiple_of(k * 512, 512)
+            stage[i % 2, pl.ds(r, 512), :] = acc[pl.ds(pl.multiple_of(i * ROWS + r, 512), 512), :].astype(jnp.bfloat16)
             return 0
-        lax.fori_loop(0, ROWS // 256, narrow, 0)
+        lax.fori_loop(0, ROWS // 512, narrow, 0)
         copy(i).start()
         return 0
     lax.fori_loop(0, OWNERS, write, 0)

time: 268 us -> 261 us (0.974)
  Pallas kernels: 231 us -> 223 us
    pallas_call x1, Pallas kernels: 41.2 us -> 37.8 us  [scatter_rows(): pl.pallas_call(scatter_kernel, out_shape=jax.ShapeDtypeStruct((TABLE, 128...]
where the time goes in v3:
time: 261 us; the launch traced here: 260 us
  Pallas kernels  223 us (85%)
  local copies, waits for them, and re-layouts  27.2 us (10%)
  other arithmetic  8.32 us (3%)
    pallas_call x1, Pallas kernels, reduce_tables(): pl.pallas_call(reduce_kernel, out_shape=jax.ShapeDtypeStruct((ROWS, 128),...  91.8 us
    pallas_call x1, Pallas kernels, gather_tables(): pl.pallas_call(gather_kernel, out_shape=jax.ShapeDtypeStruct((TABLE, 128)...  79.1 us
    pallas_call x1, Pallas kernels, scatter_rows(): pl.pallas_call(scatter_kernel, out_shape=jax.ShapeDtypeStruct((TABLE, 128...  37.8 us
    gather x1, local copies, waits for them, and re-layouts, body(): fetched = gather_tables(table_rows.astype(jnp.bfloat16))[ids]  24.5 us
    pallas_call x1, Pallas kernels, cross_layer(): pl.pallas_call(cross_kernel, out_shape=(jax.ShapeDtypeStruct((samples, 1)...  14.7 us

profile of v3, /device:TPU:1, one launch (start us, length us, event | category | flops | bytes accessed | tf_op | source)
XLA Modules:
  0.0 259.6 jit_solution(9579392638976783668)
XLA Ops:
  0.6 0.8 fusion.4
  1.4 0.1 fusion.3
  1.5 2.4 convert_element_type.6.tab
  3.9 79.1 %gather_tables.1 = bf16[98304,128]{1,0:T(8,128)(2,1)} custom-call(bf16[3072,128]{1,0:T(8,128)(2,1)} %convert_element_type.6.tab), custom_call_target="tpu_custom_call" | custom-call | bytes 50000000 | tf_op jit(solution)/shard_map/gather_tables/pallas_call | solution.py:174
  83.0 0.0 copy-start.5
  83.0 0.0 copy-start.2
  83.0 0.0 copy-start.3
  83.0 24.5 %gather_fusion = bf16[6656,128]{1,0:T(8,128)(2,1)} fusion(bf16[98304,128]{1,0:T(8,128)(2,1)} %gather_tables.1, s32[7168]{0:T(1024)S(1)} %pad_clamp_fusion), kind=kCustom, calls=%fused_computation | custom fusion | bytes 3434496 | tf_op jit(solution)/shard_map/gather | solution.py:497
  107.5 0.0 copy-done.5
  107.5 0.8 copy.14.labels
  108.3 0.0 copy-done.2
  108.3 0.6 broadcast_in_dim.12.bias
  108.9 0.0 copy-done.3
  108.9 0.6 broadcast_in_dim.13.weight
  109.5 14.7 %cross_layer.1 = (f32[256,1]{1,0:T(8,128)}, bf16[6656,128]{1,0:T(8,128)(2,1)}) custom-call(bf16[256,128]{1,0:T(8,128)(2,1)} %dense.1, bf16[6656,128]{1,0:T(8,128)(2,1)} %gather_fusion, s32[256,1]{1,0:T(8,128)} %copy.14.labels, bf16[3456,512]{1,0:T(8,128)(2,1)} %down_hbm.1, bf16[512,3456]{1,0:T(8,128)(2,1)} %up_hbm.1, f32[1,3456]{1,0:T(1,128)} %broadcast_in_dim.12.bias, ...), custom_call_target="tpu_custom_call" | custom-call | tf_op jit(solution)/shard_map/cross_layer/pallas_call | solution.py:464
  124.2 0.6 reshape.44.ids
  124.8 37.8 %scatter_rows.1.part = bf16[98304,128]{1,0:T(8,128)(2,1)} custom-call(s32[6656]{0:T(1024)} %reshape.44.ids, bf16[6656,128]{1,0:T(8,128)(2,1)} %get-tuple-element.4.g), custom_call_target="tpu_custom_call" | custom-call | tf_op jit(solution)/shard_map/scatter_rows/pallas_call | solution.py:231
  162.7 0.0 copy-start.4
  162.7 0.0 copy-start
  162.7 91.8 %reduce_tables.1 = bf16[3072,128]{1,0:T(8,128)(2,1)} custom-call(bf16[98304,128]{1,0:T(8,128)(2,1)} %scatter_rows.1.part), custom_call_target="tpu_custom_call" | custom-call | bytes 50000000 | tf_op jit(solution)/shard_map/reduce_tables/pallas_call | solution.py:390
  254.5 1.6 fusion.2
  256.1 0.0 copy-done.4
  256.1 0.0 copy-done
  256.1 0.0 copy-start.1
  256.1 2.8 %fusion.1 = f32[3072,128]{1,0:T(8,128)} fusion(f32[3072,128]{1,0:T(8,128)S(1)} %copy-done, bf16[3072,128]{1,0:T(8,128)(2,1)} %reduce_tables.1, f32[3072]{0:T(1024)S(1)} %add_sqrt_fusion), kind=kLoop, calls=%fused_computation.4 | loop fusion | flops 1572864 | bytes 3944448 | tf_op jit(solution)/shard_map/sub | solution.py:503
  258.9 0.0 copy-done.1
  258.9 0.7 reduce.1
  (3 shorter events, 0.0 us)
Async XLA Ops:
  83.0 24.6 %copy-start.5 = (s32[256]{0:T(256)S(1)}, s32[256]{0:T(256)}, u32[]{:S(2)}) copy-start(s32[256]{0:T(256)} %param.13) | copy-start | bytes 3076
  83.0 25.3 %copy-start.2 = (f32[3456]{0:T(1024)S(1)}, f32[3456]{0:T(1024)}, u32[]{:S(2)}) copy-start(f32[3456]{0:T(1024)} %param.18) | copy-start | bytes 41476
  83.0 25.9 %copy-start.3 = (f32[3456]{0:T(1024)S(1)}, f32[3456]{0:T(1024)}, u32[]{:S(2)}) copy-start(f32[3456]{0:T(1024)} %param.19) | copy-start | bytes 41476
  162.7 93.4 %copy-start.4 = (f32[3072]{0:T(1024)S(1)}, f32[3072]{0:T(1024)}, u32[]{:S(2)}) copy-start(f32[3072]{0:T(1024)} %param.15) | copy-start | bytes 36868
  162.7 93.4 %copy-start = (f32[3072,128]{1,0:T(8,128)S(1)}, f32[3072,128]{1,0:T(8,128)}, u32[]{:S(2)}) copy-start(f32[3072,128]{1,0:T(8,128)} %param.14) | copy-start | bytes 4718596
  256.1 2.8 %copy-start.1 = (f32[256,1]{1,0:T(8,128)S(1)}, f32[256,1]{1,0:T(8,128)}, u32[]{:S(2)}) copy-start(f32[256,1]{1,0:T(8,128)} %get-tuple-element.5) | copy-start | bytes 3076

commit v4 on v3

--- a/solution.py
+++ b/solution.py
@@ -98,7 +98,7 @@
         device_id=device, device_id_type=pl.DeviceIdType.MESH)
 
 
-Z_LAG = 6
+Z_LAG = 14
 
 
 def gather_kernel(tab, out, own_sem, ring_s, ring_r, sib_s, sib_r, z_s, z_r, zs_s, zs_r):
@@ -183,32 +183,80 @@
     )(tab)
 
 
-LOOKUPS = 6656
-
-
-def scatter_kernel(ids, g, out, acc, gf, stage, sem):
+NT = (((1,), (1,)), ((), ()))
+LOOKUPS, TABLES, SAMPLES, FEAT, RANK = 6656, 26, 256, 3456, 512
+WRITE = 1024
+
+
+def cross_kernel(ids, dense, fetched, labels, down_hbm, up_hbm, bias, weight, logits, out,
+                 acc, rows, stage, joined, mixed, down, up, sem, row_sem, out_sem):
+    take_down = pltpu.make_async_copy(down_hbm, down, sem.at[0])
+    take_up = pltpu.make_async_copy(up_hbm, up, sem.at[1])
+
+    def take_rows(t):
+        return pltpu.make_async_copy(
+            fetched.at[pl.ds(SAMPLES * t, SAMPLES)], joined.at[:, pl.ds(128 * (t + 1), 128)], row_sem.at[t])
+    for t in range(TABLES):
+        take_rows(t).start()
+    take_down.start()
+    take_up.start()
+    joined[:, 0:128] = dense[...]
+
     def clear(i, _):
         acc[pl.ds(pl.multiple_of(i * 1024, 1024), 1024), :] = jnp.zeros((1024, 128), jnp.float32)
         return 0
     lax.fori_loop(0, TABLE // 1024, clear, 0)
-
-    def widen(i, _):
-        r = pl.ds(pl.multiple_of(i * 128, 128), 128)
-        gf[r, :] = g[r, :].astype(jnp.float32)
+    for t in range(TABLES):
+        take_rows(t).wait()
+    take_down.wait()
+
+    def columns(i, width):
+        return pl.ds(pl.multiple_of(i * width, 128), width)
+
+    def first(i, total):
+        c = columns(i, 1152)
+        return total + jnp.dot(joined[:, c], down[c, :], preferred_element_type=jnp.float32)
+    lowrank = lax.fori_loop(0, 3, first, jnp.zeros((SAMPLES, RANK), jnp.float32)).astype(jnp.bfloat16)
+    take_up.wait()
+
+    def second(i, total):
+        c = columns(i, 384)
+        m = 1.0 + (jnp.dot(lowrank, up[:, c], preferred_element_type=jnp.float32) + bias[:, c])
+        mixed[:, c] = m
+        v = joined[:, c].astype(jnp.float32) * m * weight[:, c]
+        return total + (v[:, 0:128] + v[:, 128:256] + v[:, 256:384])
+    total = lax.fori_loop(0, 9, second, jnp.zeros((SAMPLES, 128), jnp.float32))
+    logit = jnp.sum(total, axis=1, keepdims=True)
+    logits[...] = logit
+    slope = jax.nn.sigmoid(logit) - labels[...].astype(jnp.float32)
+
+    def third(i, total):
+        c = columns(i, 1152)
+        s = (slope * weight[:, c] * joined[:, c].astype(jnp.float32)).astype(jnp.bfloat16)
+        return total + lax.dot_general(s, up[:, c], NT, preferred_element_type=jnp.float32)
+    back = lax.fori_loop(0, 3, third, jnp.zeros((SAMPLES, RANK), jnp.float32)).astype(jnp.bfloat16)
+
+    def fourth(i, _):
+        c = pl.ds(pl.multiple_of(128 + i * 256, 128), 256)
+        e = slope * weight[:, c] * mixed[:, c] + lax.dot_general(
+            back, down[c, :], NT, preferred_element_type=jnp.float32)
+        e = e.astype(jnp.bfloat16).astype(jnp.float32)
+        rows[0:SAMPLES, :] = e[:, 0:128]
+        rows[SAMPLES:2 * SAMPLES, :] = e[:, 128:256]
+
+        def add(k, _):
+            for m in range(16):
+                j = k * 16 + m
+                row = ids[i * (2 * SAMPLES) + j]
+                acc[pl.ds(row, 1), :] = acc[pl.ds(row, 1), :] + rows[pl.ds(j, 1), :]
+            return 0
+        lax.fori_loop(0, 2 * SAMPLES // 16, add, 0)
         return 0
-    lax.fori_loop(0, LOOKUPS // 128, widen, 0)
-
-    def add(i, _):
-        for k in range(16):
-            j = i * 16 + k
-            row = ids[j]
-            acc[pl.ds(row, 1), :] = acc[pl.ds(row, 1), :] + gf[pl.ds(j, 1), :]
-        return 0
-    lax.fori_loop(0, LOOKUPS // 16, add, 0)
+    lax.fori_loop(0, TABLES // 2, fourth, 0)
 
     def copy(i):
-        slot = i % 2
-        return pltpu.make_async_copy(stage.at[slot], out.at[pl.ds(pl.multiple_of(i * ROWS, ROWS), ROWS)], sem.at[slot])
+        return pltpu.make_async_copy(
+            stage.at[i % 2], out.at[pl.ds(pl.multiple_of(i * WRITE, WRITE), WRITE)], out_sem.at[i % 2])
 
     def write(i, _):
         @pl.when(i >= 2)
@@ -217,28 +265,32 @@
 
         def narrow(k, _):
             r = pl.multiple_of(k * 512, 512)
-            stage[i % 2, pl.ds(r, 512), :] = acc[pl.ds(pl.multiple_of(i * ROWS + r, 512), 512), :].astype(jnp.bfloat16)
+            stage[i % 2, pl.ds(r, 512), :] = acc[pl.ds(pl.multiple_of(i * WRITE + r, 512), 512), :].astype(jnp.bfloat16)
             return 0
-        lax.fori_loop(0, ROWS // 512, narrow, 0)
+        lax.fori_loop(0, WRITE // 512, narrow, 0)
         copy(i).start()
         return 0
-    lax.fori_loop(0, OWNERS, write, 0)
-    copy(OWNERS - 2).wait()
-    copy(OWNERS - 1).wait()
-
-
-def scatter_rows(ids, g):
+    lax.fori_loop(0, TABLE // WRITE, write, 0)
+    copy(TABLE // WRITE - 2).wait()
+    copy(TABLE // WRITE - 1).wait()
+
+
+def cross_layer(ids, dense, fetched, labels, down, up, bias, weight):
+    vmem, hbm = pl.BlockSpec(memory_space=pltpu.VMEM), pl.BlockSpec(memory_space=pl.ANY)
+    f32, bf = jnp.float32, jnp.bfloat16
     return pl.pallas_call(
-        scatter_kernel,
-        out_shape=jax.ShapeDtypeStruct((TABLE, 128), jnp.bfloat16),
-        in_specs=[pl.BlockSpec(memory_space=pltpu.SMEM), pl.BlockSpec(memory_space=pltpu.VMEM)],
-        out_specs=pl.BlockSpec(memory_space=pl.ANY),
+        cross_kernel,
+        out_shape=(jax.ShapeDtypeStruct((SAMPLES, 1), f32), jax.ShapeDtypeStruct((TABLE, 128), bf)),
+        in_specs=[pl.BlockSpec(memory_space=pltpu.SMEM), vmem, hbm, vmem, hbm, hbm, vmem, vmem],
+        out_specs=[vmem, hbm],
         scratch_shapes=[
-            pltpu.VMEM((TABLE, 128), jnp.float32), pltpu.VMEM((LOOKUPS, 128), jnp.float32),
-            pltpu.VMEM((2, ROWS, 128), jnp.bfloat16), pltpu.SemaphoreType.DMA((2,))],
-        compiler_params=pltpu.CompilerParams(vmem_limit_bytes=60 * 1024 * 1024),
-        name="scatter_rows",
-    )(ids, g)
+            pltpu.VMEM((TABLE, 128), f32), pltpu.VMEM((2 * SAMPLES, 128), f32), pltpu.VMEM((2, WRITE, 128), bf),
+            pltpu.VMEM((SAMPLES, FEAT), bf), pltpu.VMEM((SAMPLES, FEAT), f32),
+            pltpu.VMEM((FEAT, RANK), bf), pltpu.VMEM((RANK, FEAT), bf),
+            dma(2), dma(TABLES), dma(2)],
+        compiler_params=pltpu.CompilerParams(vmem_limit_bytes=63 * 1024 * 1024),
+        name="cross_layer",
+    )(ids, dense, fetched, labels, down, up, bias, weight)
 
 
 CHUNK = 128
@@ -404,77 +456,6 @@
     )(part)
 
 
-NT = (((1,), (1,)), ((), ()))
-
-
-def cross_kernel(dense, fetched, labels, down_hbm, up_hbm, bias, weight, logits, grads, joined, mixed, down, up, sem):
-    samples = dense.shape[0]
-    take_down = pltpu.make_async_copy(down_hbm, down, sem.at[0])
-    take_up = pltpu.make_async_copy(up_hbm, up, sem.at[1])
-    take_down.start()
-    take_up.start()
-    joined[:, 0:128] = dense[...]
-    for t in range(26):
-        joined[:, 128 * (t + 1):128 * (t + 2)] = fetched[samples * t:samples * (t + 1), :]
-
-    def columns(i, width):
-        return pl.ds(pl.multiple_of(i * width, 128), width)
-
-    take_down.wait()
-
-    def first(i, acc):
-        c = columns(i, 1152)
-        return acc + jnp.dot(joined[:, c], down[c, :], preferred_element_type=jnp.float32)
-    lowrank = lax.fori_loop(0, 3, first, jnp.zeros((samples, 512), jnp.float32)).astype(jnp.bfloat16)
-
-    take_up.wait()
-
-    def second(i, acc):
-        c = columns(i, 384)
-        m = 1.0 + (jnp.dot(lowrank, up[:, c], preferred_element_type=jnp.float32) + bias[:, c])
-        mixed[:, c] = m
-        v = joined[:, c].astype(jnp.float32) * m * weight[:, c]
-        return acc + (v[:, 0:128] + v[:, 128:256] + v[:, 256:384])
-    acc = lax.fori_loop(0, 9, second, jnp.zeros((samples, 128), jnp.float32))
-    logit = jnp.sum(acc, axis=1, keepdims=True)
-    logits[...] = logit
-    slope = jax.nn.sigmoid(logit) - labels[...].astype(jnp.float32)
-
-    def third(i, acc):
-        c = columns(i, 1152)
-        s = (slope * weight[:, c] * joined[:, c].astype(jnp.float32)).astype(jnp.bfloat16)
-        return acc + lax.dot_general(s, up[:, c], NT, preferred_element_type=jnp.float32)
-    back = lax.fori_loop(0, 3, third, jnp.zeros((samples, 512), jnp.float32)).astype(jnp.bfloat16)
-
-    def fourth(i, _):
-        c = pl.ds(pl.multiple_of(128 + i * 256, 128), 256)
-        e = slope * weight[:, c] * mixed[:, c] + lax.dot_general(
-            back, down[c, :], NT, preferred_element_type=jnp.float32)
-        e = e.astype(jnp.bfloat16)
-        r = pl.multiple_of(i * 2 * samples, 512)
-        grads[pl.ds(r, samples), :] = e[:, 0:128]
-        grads[pl.ds(r + samples, samples), :] = e[:, 128:256]
-        return 0
-    lax.fori_loop(0, 13, fourth, 0)
-
-
-def cross_layer(dense, fetched, labels, down, up, bias, weight):
-    samples = dense.shape[0]
-    vmem = pl.BlockSpec(memory_space=pltpu.VMEM)
-    return pl.pallas_call(
-        cross_kernel,
-        out_shape=(
-            jax.ShapeDtypeStruct((samples, 1), jnp.float32),
-            jax.ShapeDtypeStruct(fetched.shape, jnp.bfloat16)),
-        in_specs=[vmem] * 3 + [pl.BlockSpec(memory_space=pl.ANY)] * 2 + [vmem] * 2,
-        out_specs=[vmem] * 2,
-        scratch_shapes=[pltpu.VMEM((samples, 3456), jnp.bfloat16), pltpu.VMEM((samples, 3456), jnp.float32),
-                        pltpu.VMEM(down.shape, jnp.bfloat16), pltpu.VMEM(up.shape, jnp.bfloat16), dma(2)],
-        compiler_params=pltpu.CompilerParams(vmem_limit_bytes=60 * 1024 * 1024),
-        name="cross_layer",
-    )(dense, fetched, labels, down, up, bias, weight)
-
-
 learn_rate = 0.1
 
 
@@ -495,10 +476,10 @@
     lookups = samples * tables
     ids = (owner_route.reshape(samples, tables) * ROWS + local_row).T.reshape(lookups)
     fetched = gather_tables(table_rows.astype(jnp.bfloat16))[ids]
-    logits, emb_grad = cross_layer(
-        dense_input, fetched, labels[:, None], cross_down, cross_up, cross_bias[None, :], out_weight[None, :]
+    logits, partial_rows = cross_layer(
+        ids, dense_input, fetched, labels[:, None], cross_down, cross_up, cross_bias[None, :], out_weight[None, :]
     )
-    row_grad = reduce_tables(scatter_rows(ids, emb_grad)).astype(jnp.float32)
+    row_grad = reduce_tables(partial_rows).astype(jnp.float32)
     fresh_state = adagrad_state + jnp.mean(row_grad * row_grad, axis=1)
     new_rows = table_rows - learn_rate * row_grad / jnp.sqrt(fresh_state)[:, None]
     return (new_rows, logits.reshape(samples))

time: 261 us -> 275 us (1.054)
  Pallas kernels: 223 us -> 236 us
    pallas_call x2 -> x1, Pallas kernels: 52.5 us -> 69.1 us  [cross_layer(): pl.pallas_call(cross_kernel, out_shape=(jax.ShapeDtypeStruct((SAMPLES, 1)...]
where the time goes in v4:
time: 275 us
  Pallas kernels  236 us (86%)
  local copies, waits for them, and re-layouts  29.3 us (11%)
  other arithmetic  8.28 us (3%)
    pallas_call x1, Pallas kernels, reduce_tables(): pl.pallas_call(reduce_kernel, out_shape=jax.ShapeDtypeStruct((ROWS, 128),...  90.5 us
    pallas_call x1, Pallas kernels, gather_tables(): pl.pallas_call(gather_kernel, out_shape=jax.ShapeDtypeStruct((TABLE, 128)...  76.6 us
    pallas_call x1, Pallas kernels, cross_layer(): pl.pallas_call(cross_kernel, out_shape=(jax.ShapeDtypeStruct((SAMPLES, 1)...  69.1 us
    gather x1, local copies, waits for them, and re-layouts, body(): fetched = gather_tables(table_rows.astype(jnp.bfloat16))[ids]  24.5 us

profile of v4, /device:TPU:1, one launch (start us, length us, event | category | flops | bytes accessed | tf_op | source)
XLA Modules:
  0.0 274.5 jit_solution(1240198140504927065)
XLA Ops:
  0.6 1.3 broadcast_in_dim.12.bias
  2.0 1.3 broadcast_in_dim.13.weight
  3.3 0.8 fusion.4
  4.1 0.1 fusion.3
  4.2 0.6 reshape.44.ids
  4.8 1.5 copy.14.labels
  6.3 2.4 convert_element_type.6.tab
  8.6 76.6 %gather_tables.1 = bf16[98304,128]{1,0:T(8,128)(2,1)} custom-call(bf16[3072,128]{1,0:T(8,128)(2,1)} %convert_element_type.6.tab), custom_call_target="tpu_custom_call" | custom-call | bytes 50000000 | tf_op jit(solution)/shard_map/gather_tables/pallas_call | solution.py:174
  85.3 24.5 %gather_fusion = bf16[6656,128]{1,0:T(8,128)(2,1)} fusion(bf16[98304,128]{1,0:T(8,128)(2,1)} %gather_tables.1, s32[7168]{0:T(1024)S(1)} %pad_clamp_fusion), kind=kCustom, calls=%fused_computation | custom fusion | bytes 3434496 | tf_op jit(solution)/shard_map/gather | solution.py:478
  109.8 69.1 %cross_layer.1 = (f32[256,1]{1,0:T(8,128)}, bf16[98304,128]{1,0:T(8,128)(2,1)}) custom-call(s32[6656]{0:T(1024)} %reshape.44.ids, bf16[256,128]{1,0:T(8,128)(2,1)} %dense.1, bf16[6656,128]{1,0:T(8,128)(2,1)} %gather_fusion, s32[256,1]{1,0:T(8,128)} %copy.14.labels, bf16[3456,512]{1,0:T(8,128)(2,1)} %down_hbm.1, bf16[512,3456]{1,0:T(8,128)(2,1)} %up_hbm.1, ...), custom_call_target="tpu_custom_call" | custom-call | tf_op jit(solution)/shard_map/cross_layer/pallas_call | solution.py:281
  178.9 0.0 copy-start.1
  178.9 0.0 copy-start.2
  178.9 0.0 copy-start
  178.9 90.5 %reduce_tables.1 = bf16[3072,128]{1,0:T(8,128)(2,1)} custom-call(bf16[98304,128]{1,0:T(8,128)(2,1)} %get-tuple-element.4.part), custom_call_target="tpu_custom_call" | custom-call | bytes 50000000 | tf_op jit(solution)/shard_map/reduce_tables/pallas_call | solution.py:442
  269.4 0.0 copy-done.1
  269.4 0.7 reduce.1
  270.1 1.6 fusion.2
  271.7 0.0 copy-done.2
  271.8 0.0 copy-done
  271.8 2.8 %fusion.1 = f32[3072,128]{1,0:T(8,128)} fusion(f32[3072,128]{1,0:T(8,128)S(1)} %copy-done, bf16[3072,128]{1,0:T(8,128)(2,1)} %reduce_tables.1, f32[3072]{0:T(1024)S(1)} %add_sqrt_fusion), kind=kLoop, calls=%fused_computation.4 | loop fusion | flops 1572864 | bytes 3944448 | tf_op jit(solution)/shard_map/sub | solution.py:484
  (3 shorter events, 0.0 us)
Async XLA Ops:
  178.9 90.6 %copy-start.1 = (f32[256,1]{1,0:T(8,128)S(1)}, f32[256,1]{1,0:T(8,128)}, u32[]{:S(2)}) copy-start(f32[256,1]{1,0:T(8,128)} %get-tuple-element.5) | copy-start | bytes 3076
  178.9 92.8 %copy-start.2 = (f32[3072]{0:T(1024)S(1)}, f32[3072]{0:T(1024)}, u32[]{:S(2)}) copy-start(f32[3072]{0:T(1024)} %param.15) | copy-start | bytes 36868
  178.9 92.9 %copy-start = (f32[3072,128]{1,0:T(8,128)S(1)}, f32[3072,128]{1,0:T(8,128)}, u32[]{:S(2)}) copy-start(f32[3072,128]{1,0:T(8,128)} %param.14) | copy-start | bytes 4718596

commit v5 on v3

--- a/solution.py
+++ b/solution.py
@@ -98,7 +98,7 @@
         device_id=device, device_id_type=pl.DeviceIdType.MESH)
 
 
-Z_LAG = 6
+Z_LAG = 14
 
 
 def gather_kernel(tab, out, own_sem, ring_s, ring_r, sib_s, sib_r, z_s, z_r, zs_s, zs_r):
@@ -242,7 +242,7 @@
 
 
 CHUNK = 128
-LOAD_AHEAD, Z_AHEAD = 20, 10
+LOAD_AHEAD, Z_AHEAD = 20, 14
 BACK = [e for e in reversed(ORDER)] + [(0, 0), (1, 0)]
 
 

time: 261 us -> 256 us (0.981)
  Pallas kernels: 223 us -> 220 us
where the time goes in v5:
time: 256 us
  Pallas kernels  220 us (86%)
  local copies, waits for them, and re-layouts  27.2 us (11%)
  other arithmetic  8.32 us (3%)
    pallas_call x1, Pallas kernels, reduce_tables(): pl.pallas_call(reduce_kernel, out_shape=jax.ShapeDtypeStruct((ROWS, 128),...  90.5 us
    pallas_call x1, Pallas kernels, gather_tables(): pl.pallas_call(gather_kernel, out_shape=jax.ShapeDtypeStruct((TABLE, 128)...  76.6 us
    pallas_call x1, Pallas kernels, scatter_rows(): pl.pallas_call(scatter_kernel, out_shape=jax.ShapeDtypeStruct((TABLE, 128...  37.8 us
    gather x1, local copies, waits for them, and re-layouts, body(): fetched = gather_tables(table_rows.astype(jnp.bfloat16))[ids]  24.5 us
    pallas_call x1, Pallas kernels, cross_layer(): pl.pallas_call(cross_kernel, out_shape=(jax.ShapeDtypeStruct((samples, 1)...  14.7 us

profile of v5, /device:TPU:1, one launch (start us, length us, event | category | flops | bytes accessed | tf_op | source)
XLA Modules:
  0.0 255.9 jit_solution(14345737411624877023)
XLA Ops:
  0.6 0.8 fusion.4
  1.4 0.1 fusion.3
  1.5 2.4 convert_element_type.6.tab
  3.9 76.6 %gather_tables.1 = bf16[98304,128]{1,0:T(8,128)(2,1)} custom-call(bf16[3072,128]{1,0:T(8,128)(2,1)} %convert_element_type.6.tab), custom_call_target="tpu_custom_call" | custom-call | bytes 50000000 | tf_op jit(solution)/shard_map/gather_tables/pallas_call | solution.py:174
  80.6 0.0 copy-start.5
  80.6 0.0 copy-start.2
  80.6 0.0 copy-start.3
  80.6 24.5 %gather_fusion = bf16[6656,128]{1,0:T(8,128)(2,1)} fusion(bf16[98304,128]{1,0:T(8,128)(2,1)} %gather_tables.1, s32[7168]{0:T(1024)S(1)} %pad_clamp_fusion), kind=kCustom, calls=%fused_computation | custom fusion | bytes 3434496 | tf_op jit(solution)/shard_map/gather | solution.py:497
  105.1 0.0 copy-done.5
  105.1 0.8 copy.14.labels
  105.9 0.0 copy-done.2
  105.9 0.6 broadcast_in_dim.12.bias
  106.5 0.0 copy-done.3
  106.5 0.6 broadcast_in_dim.13.weight
  107.1 14.7 %cross_layer.1 = (f32[256,1]{1,0:T(8,128)}, bf16[6656,128]{1,0:T(8,128)(2,1)}) custom-call(bf16[256,128]{1,0:T(8,128)(2,1)} %dense.1, bf16[6656,128]{1,0:T(8,128)(2,1)} %gather_fusion, s32[256,1]{1,0:T(8,128)} %copy.14.labels, bf16[3456,512]{1,0:T(8,128)(2,1)} %down_hbm.1, bf16[512,3456]{1,0:T(8,128)(2,1)} %up_hbm.1, f32[1,3456]{1,0:T(1,128)} %broadcast_in_dim.12.bias, ...), custom_call_target="tpu_custom_call" | custom-call | tf_op jit(solution)/shard_map/cross_layer/pallas_call | solution.py:464
  121.8 0.6 reshape.44.ids
  122.4 37.8 %scatter_rows.1.part = bf16[98304,128]{1,0:T(8,128)(2,1)} custom-call(s32[6656]{0:T(1024)} %reshape.44.ids, bf16[6656,128]{1,0:T(8,128)(2,1)} %get-tuple-element.4.g), custom_call_target="tpu_custom_call" | custom-call | tf_op jit(solution)/shard_map/scatter_rows/pallas_call | solution.py:231
  160.3 0.0 copy-start.4
  160.3 0.0 copy-start
  160.3 90.5 %reduce_tables.1 = bf16[3072,128]{1,0:T(8,128)(2,1)} custom-call(bf16[98304,128]{1,0:T(8,128)(2,1)} %scatter_rows.1.part), custom_call_target="tpu_custom_call" | custom-call | bytes 50000000 | tf_op jit(solution)/shard_map/reduce_tables/pallas_call | solution.py:390
  250.8 1.6 fusion.2
  252.4 0.0 copy-done.4
  252.4 0.0 copy-done
  252.4 0.0 copy-start.1
  252.4 2.8 %fusion.1 = f32[3072,128]{1,0:T(8,128)} fusion(f32[3072,128]{1,0:T(8,128)S(1)} %copy-done, bf16[3072,128]{1,0:T(8,128)(2,1)} %reduce_tables.1, f32[3072]{0:T(1024)S(1)} %add_sqrt_fusion), kind=kLoop, calls=%fused_computation.4 | loop fusion | flops 1572864 | bytes 3944448 | tf_op jit(solution)/shard_map/sub | solution.py:503
  255.2 0.0 copy-done.1
  255.2 0.7 reduce.1
  (3 shorter events, 0.0 us)
Async XLA Ops:
  80.6 24.6 %copy-start.5 = (s32[256]{0:T(256)S(1)}, s32[256]{0:T(256)}, u32[]{:S(2)}) copy-start(s32[256]{0:T(256)} %param.13) | copy-start | bytes 3076
  80.6 25.3 %copy-start.2 = (f32[3456]{0:T(1024)S(1)}, f32[3456]{0:T(1024)}, u32[]{:S(2)}) copy-start(f32[3456]{0:T(1024)} %param.18) | copy-start | bytes 41476
  80.6 25.9 %copy-start.3 = (f32[3456]{0:T(1024)S(1)}, f32[3456]{0:T(1024)}, u32[]{:S(2)}) copy-start(f32[3456]{0:T(1024)} %param.19) | copy-start | bytes 41476
  160.3 92.1 %copy-start.4 = (f32[3072]{0:T(1024)S(1)}, f32[3072]{0:T(1024)}, u32[]{:S(2)}) copy-start(f32[3072]{0:T(1024)} %param.15) | copy-start | bytes 36868
  160.3 92.1 %copy-start = (f32[3072,128]{1,0:T(8,128)S(1)}, f32[3072,128]{1,0:T(8,128)}, u32[]{:S(2)}) copy-start(f32[3072,128]{1,0:T(8,128)} %param.14) | copy-start | bytes 4718596
  252.4 2.8 %copy-start.1 = (f32[256,1]{1,0:T(8,128)S(1)}, f32[256,1]{1,0:T(8,128)}, u32[]{:S(2)}) copy-start(f32[256,1]{1,0:T(8,128)} %get-tuple-element.5) | copy-start | bytes 3076
